TPU v7x, 32 devices: a whole 2x2x4 slice. The times are simulated.
32 devices in a mesh: group: 2 (over x), mod: 4 (over y, core), dir: 4 (over z).
Axes of the slice: x: 2, y: 2, z: 4, core: 2. Of those that a mesh axis runs over, the one named last changes fastest.
Arguments:
- screens: float32 [8, 512, 512], P('group', 'mod'), parts along dimension 0, may hold values from -6 to 6
- footprint: int32 [8, 4, 2], P(('group', 'dir')), parts along dimension 0, may hold values from 0 to 191
- fraction: int32 [8, 4, 2], P(('group', 'dir')), parts along dimension 0, may hold values from 0 to 15
- tilt_steps: int32 [16, 2], P(('group', 'mod')), parts along dimension 0, may hold values from -64 to 64
- facet_shift: int32 [4, 2], replicated, may hold values from 80 to 160
Outputs:
- detector: float32 [8, 640, 640], P(('group', 'dir'), 'mod'), parts along dimension 0
There are 2 independent parts, one for each index of `group`. A program takes and returns all parts, laid end to end along the dimension named above; an argument that names none is the same for every part. Nothing has to cross between parts.
All inputs are finite; a program needn't handle non-finite values.
Results may differ from a plain program's by a relative error of at most 0.0055.
Values may be sent and summed in bfloat16 or wider, within the bound.
No kernel may reach another device: no remote copies, remote signals or barrier semaphores. Data moves between devices by JAX's collectives and lax.ppermute only.
A program may use at most 64 MiB of HBM per device.

v0:
```python
import functools

import jax
import jax.numpy as jnp
from jax import lax
from jax.experimental import pallas as pl
from jax.experimental.pallas import tpu as pltpu
from jax.sharding import PartitionSpec as P

P_SIZE = 320
PAD = 640
HALF = P_SIZE // 2
FINE = 8 * PAD
CENTRE = 2 * (PAD - 2)
F32 = jnp.float32
BF16 = jnp.bfloat16
I32 = jnp.int32
I16 = jnp.int16
SIN_TERMS = (6.283184916, -41.34158923, 81.59994333, -76.61447253, 41.34288235, -12.47124354)
COS_TERMS = (0.9999992108, -19.73898036, 64.92865742, -85.27162153, 58.79049212, -21.07110563)


def round_up(value, step):
    return (value + step - 1) // step * step


def horner(terms, square):
    total = jnp.full_like(square, terms[-1])
    for term in terms[-2::-1]:
        total = total * square + term
    return total


def cos_sin(turns):
    square = turns * turns
    return horner(COS_TERMS, square), horner(SIN_TERMS, square) * turns


def centred(turns):
    return turns - jnp.floor(turns + 0.5)


def iota(shape, axis):
    return lax.broadcasted_iota(I32, shape, axis)


def lane_vector(values, index):
    out = jnp.zeros(index.shape, values[0].dtype)
    for place, value in enumerate(values):
        out = jnp.where(index == place, value, out)
    return out


def phase_kernel(foot, frac, tilt, screens, keep, send, *, lanes):
    layers, band, width = screens.shape
    points = tilt.shape[0]
    me = lax.axis_index("mod")
    high, low = [], []
    for layer in range(layers):
        start = foot[0, layer, 1]
        part = frac[0, layer, 1].astype(F32) * (1.0 / 16.0)
        rows = screens[layer]
        here = pltpu.roll(rows, lax.rem(width - start, width), 1)[:, :lanes]
        after = pltpu.roll(rows, width - 1 - start, 1)[:, :lanes]
        mixed = here * (1.0 - part) + after * part
        top = mixed.astype(BF16)
        high.append(top)
        low.append((mixed - top.astype(F32)).astype(BF16))
    index = iota((1, layers * band), 1)
    layer_of = index // band
    first = lane_vector([foot[0, i, 0] for i in range(layers)], layer_of)
    part = lane_vector([frac[0, i, 0].astype(F32) * (1.0 / 16.0) for i in range(layers)], layer_of)
    offset = me * band + index - layer_of * band - first
    delta = offset - iota((P_SIZE, layers * band), 0)
    pick = jnp.where(delta == 0, 1.0 - part, jnp.where(delta == 1, part, 0.0)).astype(BF16)
    total = jnp.dot(pick, jnp.concatenate(high, 0), preferred_element_type=F32)
    total = total + jnp.dot(pick, jnp.concatenate(low, 0), preferred_element_type=F32)
    coded = jnp.floor(total * (65536.0 / 6.283185307179586) + 0.5).astype(I32)
    coded = lax.shift_right_arithmetic(lax.shift_left(coded, 16), 16)
    row = iota((HALF, lanes), 0)
    lane = iota((HALF, lanes), 1)
    table = jnp.zeros((HALF, lanes), I32)
    for point in range(points):
        place = me * points + point
        table = jnp.where((lane == P_SIZE + place) & (row == HALF - 1), tilt[point, 0], table)
        table = jnp.where((lane == lanes - 1) & (row == place), tilt[point, 1], table)
    upper = jnp.where(lane < P_SIZE, coded[:HALF], table)
    lower = jnp.where(lane < P_SIZE, coded[HALF:], table)
    odd = lax.rem(me, 2) == 1
    keep[...] = jnp.where(odd, lower, upper).astype(I16)
    send[...] = jnp.where(odd, upper, lower).astype(I16)


def dirichlet(steps, flip):
    size = jnp.abs(steps)
    near = jnp.minimum(size, PAD - size)
    turns = near.astype(F32) * (0.5 / PAD)
    sine = horner(SIN_TERMS, turns * turns) * turns
    quarter = jnp.bitwise_and(steps, 3)
    negative = (quarter == 3) != ((steps < 0) != flip)
    value = 1.0 / (jnp.where(negative, -float(PAD), float(PAD)) * sine)
    odd = jnp.bitwise_and(steps, 1) == 1
    return jnp.where(odd, value, jnp.where(steps == 0, 0.5, 0.0)).astype(BF16)


def shift_of(facet, quadrant, axis):
    side = quadrant // 2 if axis == 0 else quadrant % 2
    return facet[quadrant, axis] * (2 * side - 1), side == 0


def table_kernel(facet, left, right, *, rows, padded, lanes):
    first = lax.axis_index("mod") * rows
    for quadrant in range(4):
        shift, flip = shift_of(facet, quadrant, 0)
        steps = iota((padded, P_SIZE), 0) - iota((padded, P_SIZE), 1) + (first - HALF - shift)
        left[pl.ds(quadrant * padded, padded), :] = dirichlet(steps, flip)
        shift, flip = shift_of(facet, quadrant, 1)
        source = iota((lanes, PAD), 0)
        steps = iota((lanes, PAD), 1) - source + (-HALF - shift)
        value = dirichlet(steps, flip)
        right[pl.ds(quadrant * lanes, lanes), :] = jnp.where(source < P_SIZE, value, 0.0).astype(BF16)


def image_kernel(
    facet, own, other, left, right, out, row_re, row_im, col_re, col_im, field_re, field_im, total, *, count, padded, lanes
):
    me = lax.axis_index("mod")
    odd = lax.rem(me, 2) == 1
    mine = own[...].astype(I32)
    theirs = other[...].astype(I32)
    coded = jnp.concatenate([jnp.where(odd, theirs, mine), jnp.where(odd, mine, theirs)], 0)
    wave_re, wave_im = cos_sin(coded.astype(F32) * (1.0 / 65536.0))
    along_y = 2 * iota((P_SIZE, lanes), 0) - (P_SIZE - 1)
    along_x = 2 * iota((P_SIZE, lanes), 1) - (P_SIZE - 1)
    radius = along_y * along_y + along_x * along_x
    edge = P_SIZE * 28 // 100
    inside = (radius <= P_SIZE * P_SIZE) & (radius >= edge * edge)
    field_re[...] = jnp.where(inside, wave_re, 0.0)
    field_im[...] = jnp.where(inside, wave_im, 0.0)
    base = P_SIZE // 128 * 128
    tilt_row = mine[HALF - 1 : HALF, base : base + 128]
    steps = (tilt_row - CENTRE) * iota((P_SIZE, 128), 0)
    cos_rows, sin_rows = cos_sin(centred(steps.astype(F32) * (1.0 / FINE)))
    for point in range(count):
        place = P_SIZE - base + point
        row_re[point] = jnp.broadcast_to(cos_rows[:, place : place + 1], (P_SIZE, 128))
        row_im[point] = jnp.broadcast_to(sin_rows[:, place : place + 1], (P_SIZE, 128))
    quad = iota((8, 1), 0)
    facet_steps = jnp.zeros((8, 1), I32)
    for quadrant in range(4):
        shift = shift_of(facet, quadrant, 0)[0] + shift_of(facet, quadrant, 1)[0]
        facet_steps = jnp.where(quad == quadrant, shift * (-2 * (PAD - 2)), facet_steps)
    for point in range(count):
        tilt_col = mine[point : point + 1, lanes - 1 : lanes]
        steps = (tilt_col - CENTRE) * iota((8, lanes), 1) + facet_steps
        turn_re, turn_im = cos_sin(centred(steps.astype(F32) * (1.0 / FINE)))
        col_re[point] = turn_re
        col_im[point] = turn_im
    total[...] = jnp.zeros_like(total)

    def one_point(point, carry):
        copies = lanes // 128
        turn_re = jnp.concatenate([row_re[point]] * copies, 1)
        turn_im = jnp.concatenate([row_im[point]] * copies, 1)
        wide_re, wide_im = field_re[...], field_im[...]
        moved_re = (wide_re * turn_re - wide_im * turn_im).astype(BF16)
        moved_im = (wide_re * turn_im + wide_im * turn_re).astype(BF16)
        half = jnp.dot(left[...], jnp.concatenate([moved_re, moved_im], 1), preferred_element_type=F32)
        parts_re, parts_im = [], []
        for quadrant in range(4):
            piece = half[quadrant * padded : (quadrant + 1) * padded]
            piece_re, piece_im = piece[:, :lanes], piece[:, lanes:]
            turn_re = col_re[point, quadrant : quadrant + 1, :]
            turn_im = col_im[point, quadrant : quadrant + 1, :]
            parts_re.append((piece_re * turn_re - piece_im * turn_im).astype(BF16))
            parts_im.append((piece_re * turn_im + piece_im * turn_re).astype(BF16))
        stacked = jnp.concatenate([jnp.concatenate(parts_re, 1), jnp.concatenate(parts_im, 1)], 0)
        image = jnp.dot(stacked, right[...], preferred_element_type=F32)
        image_re, image_im = image[:padded], image[padded:]
        total[...] += image_re * image_re + image_im * image_im
        return carry

    lax.fori_loop(0, count, one_point, 0)
    out[0] = total[: out.shape[1]] * (4.0 / count)


def swapped(values, peers, step):
    return lax.ppermute(values, "mod", [(i, i ^ step) for i in range(peers)])


def shards(screens, footprint, fraction, tilt_steps, facet_shift):
    peers = lax.axis_size("mod")
    layers, band, width = screens.shape
    count = tilt_steps.shape[0] * peers
    rows = PAD // peers
    padded = round_up(rows, 16)
    lanes = round_up(P_SIZE + count + 1, 128)
    smem = pl.BlockSpec(memory_space=pltpu.SMEM)
    vmem = pl.BlockSpec(memory_space=pltpu.VMEM)
    params = pltpu.CompilerParams(vmem_limit_bytes=40 * 1024 * 1024)
    half_shape = jax.ShapeDtypeStruct((HALF, lanes), I16)
    keep, send = pl.pallas_call(
        functools.partial(phase_kernel, lanes=lanes),
        out_shape=(half_shape, half_shape),
        in_specs=[smem, smem, smem, vmem],
        out_specs=(vmem, vmem),
        compiler_params=params,
        name="phase_parts",
    )(footprint, fraction, tilt_steps, screens)
    left, right = pl.pallas_call(
        functools.partial(table_kernel, rows=rows, padded=padded, lanes=lanes),
        out_shape=(
            jax.ShapeDtypeStruct((4 * padded, P_SIZE), BF16),
            jax.ShapeDtypeStruct((4 * lanes, PAD), BF16),
        ),
        in_specs=[smem],
        out_specs=(vmem, vmem),
        compiler_params=params,
        cost_estimate=pl.CostEstimate(flops=30_000_000, bytes_accessed=2_500_000, transcendentals=0),
        name="half_band_tables",
    )(facet_shift)
    own = keep + swapped(send, peers, 1)
    step = 2
    while step < peers:
        own = own + swapped(own, peers, step)
        step *= 2
    other = swapped(own, peers, 1)
    return pl.pallas_call(
        functools.partial(image_kernel, count=count, padded=padded, lanes=lanes),
        out_shape=jax.ShapeDtypeStruct((1, rows, PAD), F32),
        in_specs=[smem, vmem, vmem, vmem, vmem],
        out_specs=vmem,
        scratch_shapes=[
            pltpu.VMEM((count, P_SIZE, 128), F32),
            pltpu.VMEM((count, P_SIZE, 128), F32),
            pltpu.VMEM((count, 8, lanes), F32),
            pltpu.VMEM((count, 8, lanes), F32),
            pltpu.VMEM((P_SIZE, lanes), F32),
            pltpu.VMEM((P_SIZE, lanes), F32),
            pltpu.VMEM((padded, PAD), F32),
        ],
        compiler_params=params,
        name="detector_rows",
    )(facet_shift, own, other, left, right)


def solution(mesh):
    placed = (
        P("group", "mod", None),
        P(("group", "dir"), None, None),
        P(("group", "dir"), None, None),
        P(("group", "mod"), None),
        P(),
    )
    return jax.shard_map(
        shards,
        mesh=mesh,
        in_specs=placed,
        out_specs=P(("group", "dir"), "mod", None),
        check_vma=False,
    )
```

profile of v0, /device:TPU:0, one launch (start us, length us, event | category | flops | bytes accessed | tf_op | source)
XLA Modules:
  0.0 38.6 jit_solution(1580587240084562494)
XLA Ops:
  0.0 0.8 %copy.6.foot = s32[1,4,2]{2,1,0:T(4,128)S(1)} copy(s32[1,4,2]{1,2,0:T(2,128)} %param.6) | data formatting | bytes 64 | tf_op args[1]
  0.8 0.8 %copy.7.frac = s32[1,4,2]{2,1,0:T(4,128)S(1)} copy(s32[1,4,2]{1,2,0:T(2,128)} %param.7) | data formatting | bytes 64 | tf_op args[2]
  1.5 0.0 copy-start
  1.5 1.2 %copy-done = f32[4,128,512]{2,1,0:T(8,128)S(1)} copy-done((f32[4,128,512]{2,1,0:T(8,128)S(1)}, f32[4,128,512]{2,1,0:T(8,128)}, u32[]{:S(2)}) %copy-start) | copy-done | bytes 1048600
  2.8 0.0 copy-start.1
  2.8 0.7 %copy-done.1 = s32[2,2]{1,0:T(2,128)S(1)} copy-done((s32[2,2]{1,0:T(2,128)S(1)}, s32[2,2]{1,0:T(2,128)}, u32[]{:S(2)}) %copy-start.1) | copy-done | bytes 40
  3.4 1.7 %phase_parts.1 = (s16[160,384]{1,0:T(8,128)(2,1)S(1)}, s16[160,384]{1,0:T(8,128)(2,1)S(1)}) custom-call(s32[1,4,2]{2,1,0:T(4,128)S(1)} %copy.6.foot, s32[1,4,2]{2,1,0:T(4,128)S(1)} %copy.7.frac, s32[2,2]{1,0:T(2,128)S(1)} %copy-done.1, f32[4,128,512]{2,1,0:T(8,128)S(1)} %copy-done), custom_call_target="tpu_custom_call" | custom-call | tf_op jit(solution)/shard_map/phase_parts/pallas_call | solution.py:202
  5.1 0.5 %collective-permute-start = (s16[160,384]{1,0:T(8,128)(2,1)S(1)}, s16[160,384]{1,0:T(8,128)(2,1)S(1)}, u32[]{:S(2)}, u32[]{:S(2)}) collective-permute-start(s16[160,384]{1,0:T(8,128)(2,1)S(1)} %get-tuple-element.10), channel_id=1, source_target_pairs={{0,4},{4,0},{8,12},{12,8},{1,5},{5,1},{9,13},{13,9},{2,6},{6,2},{1... | collective-permute-start | bytes 368648 | tf_op jit(solution)/shard_map/ppermute | solution.py:188
  5.7 1.0 %collective-permute-done = s16[160,384]{1,0:T(8,128)(2,1)S(1)} collective-permute-done((s16[160,384]{1,0:T(8,128)(2,1)S(1)}, s16[160,384]{1,0:T(8,128)(2,1)S(1)}, u32[]{:S(2)}, u32[]{:S(2)}) %collective-permute-start) | collective-permute-done | bytes 122912 | tf_op jit(solution)/shard_map/ppermute | solution.py:188
  6.7 2.9 %collective-permute-start.1 = (s16[160,384]{1,0:T(8,128)(2,1)S(1)}, s16[160,384]{1,0:T(8,128)(2,1)S(1)}, u32[]{:S(2)}, u32[]{:S(2)}) collective-permute-start(s16[160,384]{1,0:T(8,128)(2,1)S(1)} %add.6), channel_id=1, source_target_pairs={{0,8},{4,12},{8,0},{12,4},{1,9},{5,13},{9,1},{13,5},{2,10},{6,14},... | collective-permute-start | bytes 368648 | tf_op jit(solution)/shard_map/ppermute | solution.py:188
  9.6 3.6 %collective-permute-done.1 = s16[160,384]{1,0:T(8,128)(2,1)S(1)} collective-permute-done((s16[160,384]{1,0:T(8,128)(2,1)S(1)}, s16[160,384]{1,0:T(8,128)(2,1)S(1)}, u32[]{:S(2)}, u32[]{:S(2)}) %collective-permute-start.1) | collective-permute-done | bytes 122912 | tf_op jit(solution)/shard_map/ppermute | solution.py:188
  13.3 0.1 collective-permute-start.2
  13.4 0.8 %copy.9.facet = s32[4,2]{1,0:T(4,128)S(1)} copy(s32[4,2]{0,1:T(2,128)} %param.9) | data formatting | bytes 64 | tf_op args[4]
  14.1 5.8 %half_band_tables.1 = (bf16[640,320]{1,0:T(8,128)(2,1)S(1)}, bf16[1536,640]{1,0:T(8,128)(2,1)S(1)}) custom-call(s32[4,2]{1,0:T(4,128)S(1)} %copy.9.facet), custom_call_target="tpu_custom_call" | custom-call | flops 30000000 | bytes 2500000 | tf_op jit(solution)/shard_map/half_band_tables/pallas_call | solution.py:210
  20.0 0.0 collective-permute-done.2.other
  20.0 18.7 %detector_rows.1 = f32[1,160,640]{2,1,0:T(8,128)} custom-call(s32[4,2]{1,0:T(4,128)S(1)} %copy.9.facet, s16[160,384]{1,0:T(8,128)(2,1)S(1)} %add.7.own, s16[160,384]{1,0:T(8,128)(2,1)S(1)} %collective-permute-done.2.other, bf16[640,320]{1,0:T(8,128)(2,1)S(1)} %get-tuple-element.11.left, bf16[1536,640]{1,0:T(8,128)(2,1)S(1)} %get-tuple-element.12.right), custom_call_target="tpu_custom_call" | custom-call | tf_op jit(solution)/shard_map/detector_rows/pallas_call | solution.py:228
  (2 shorter events, 0.1 us)
Async XLA Ops:
  1.5 1.2 %copy-start = (f32[4,128,512]{2,1,0:T(8,128)S(1)}, f32[4,128,512]{2,1,0:T(8,128)}, u32[]{:S(2)}) copy-start(f32[4,128,512]{2,1,0:T(8,128)} %screens.1) | copy-start | bytes 3145732
  2.8 0.7 %copy-start.1 = (s32[2,2]{1,0:T(2,128)S(1)}, s32[2,2]{1,0:T(2,128)}, u32[]{:S(2)}) copy-start(s32[2,2]{1,0:T(2,128)} %tilt.1) | copy-start | bytes 52
  5.1 1.5 %collective-permute-start = (s16[160,384]{1,0:T(8,128)(2,1)S(1)}, s16[160,384]{1,0:T(8,128)(2,1)S(1)}, u32[]{:S(2)}, u32[]{:S(2)}) collective-permute-start(s16[160,384]{1,0:T(8,128)(2,1)S(1)} %get-tuple-element.10), channel_id=1, source_target_pairs={{0,4},{4,0},{8,12},{12,8},{1,5},{5,1},{9,13},{13,9},{2,6},{6,2},{1... | collective-permute-start | bytes 368648 | tf_op jit(solution)/shard_map/ppermute | solution.py:188
  6.7 6.6 %collective-permute-start.1 = (s16[160,384]{1,0:T(8,128)(2,1)S(1)}, s16[160,384]{1,0:T(8,128)(2,1)S(1)}, u32[]{:S(2)}, u32[]{:S(2)}) collective-permute-start(s16[160,384]{1,0:T(8,128)(2,1)S(1)} %add.6), channel_id=1, source_target_pairs={{0,8},{4,12},{8,0},{12,4},{1,9},{5,13},{9,1},{13,5},{2,10},{6,14},... | collective-permute-start | bytes 368648 | tf_op jit(solution)/shard_map/ppermute | solution.py:188
  13.3 6.7 %collective-permute-start.2 = (s16[160,384]{1,0:T(8,128)(2,1)S(1)}, s16[160,384]{1,0:T(8,128)(2,1)S(1)}, u32[]{:S(2)}, u32[]{:S(2)}) collective-permute-start(s16[160,384]{1,0:T(8,128)(2,1)S(1)} %add.7.own), channel_id=1, source_target_pairs={{0,4},{4,0},{8,12},{12,8},{1,5},{5,1},{9,13},{13,9},{2,6},{6,2},{1... | collective-permute-start | bytes 368648 | tf_op jit(solution)/shard_map/ppermute | solution.py:188
where the time goes:
time: 38.9 us; the launch traced here: 38.6 us
  Pallas kernels  26.2 us (67%)
  waiting for transfers between devices  4.61 us (12%)
  local copies, waits for them, and re-layouts  4.2 us (11%)
  starting transfers between devices  3.53 us (9%)
    pallas_call x1, Pallas kernels, shards(): pl.pallas_call(functools.partial(image_kernel, count=count, padded=padded...  18.7 us
    pallas_call x1, Pallas kernels, shards(): pl.pallas_call(functools.partial(table_kernel, rows=rows, padded=padded,...  5.83 us
    ppermute x3, waiting for transfers between devices, swapped(): return lax.ppermute(values, 'mod', [(i, i ^ step) for i in range(peers)])  4.61 us
    unnamed x7, local copies, waits for them, and re-layouts  4.2 us
    ppermute x3, starting transfers between devices, swapped(): return lax.ppermute(values, 'mod', [(i, i ^ step) for i in range(peers)])  3.53 us
    pallas_call x1, Pallas kernels, shards(): pl.pallas_call(functools.partial(phase_kernel, lanes=lanes), out_shape=(h...  1.69 us
  transfers between devices with their start and end apart: 3, of which 2 were waited for; matrix products, arithmetic and copies ran while one was open for 2% of the time, Pallas kernels for 15%

commit v1 on v0

--- a/solution.py
+++ b/solution.py
@@ -2,6 +2,7 @@
 
 import jax
 import jax.numpy as jnp
+import numpy as np
 from jax import lax
 from jax.experimental import pallas as pl
 from jax.experimental.pallas import tpu as pltpu
@@ -51,14 +52,36 @@
     return out
 
 
-def phase_kernel(foot, frac, tilt, screens, keep, send, *, lanes):
+def phase_kernel(
+    foot_hbm, frac_hbm, tilt_hbm, screens_hbm, keep, send, foot, frac, tilt, screens, small_sems, layer_sems, *, lanes
+):
     layers, band, width = screens.shape
     points = tilt.shape[0]
     me = lax.axis_index("mod")
+    small = [
+        pltpu.make_async_copy(source, target, small_sems.at[place])
+        for place, (source, target) in enumerate(((foot_hbm, foot), (frac_hbm, frac), (tilt_hbm, tilt)))
+    ]
+    large = [
+        pltpu.make_async_copy(screens_hbm.at[layer], screens.at[layer], layer_sems.at[layer])
+        for layer in range(layers)
+    ]
+    for copy in small + large:
+        copy.start()
+    for copy in small:
+        copy.wait()
+    index = iota((1, layers * band), 1)
+    layer_of = index // band
+    first = lane_vector([foot[0, 0, i] for i in range(layers)], layer_of)
+    part = lane_vector([frac[0, 0, i].astype(F32) * (1.0 / 16.0) for i in range(layers)], layer_of)
+    offset = me * band + index - layer_of * band - first
+    delta = offset - iota((P_SIZE, layers * band), 0)
+    pick = jnp.where(delta == 0, 1.0 - part, jnp.where(delta == 1, part, 0.0)).astype(BF16)
     high, low = [], []
     for layer in range(layers):
-        start = foot[0, layer, 1]
-        part = frac[0, layer, 1].astype(F32) * (1.0 / 16.0)
+        start = foot[0, 1, layer]
+        part = frac[0, 1, layer].astype(F32) * (1.0 / 16.0)
+        large[layer].wait()
         rows = screens[layer]
         here = pltpu.roll(rows, lax.rem(width - start, width), 1)[:, :lanes]
         after = pltpu.roll(rows, width - 1 - start, 1)[:, :lanes]
@@ -66,13 +89,6 @@
         top = mixed.astype(BF16)
         high.append(top)
         low.append((mixed - top.astype(F32)).astype(BF16))
-    index = iota((1, layers * band), 1)
-    layer_of = index // band
-    first = lane_vector([foot[0, i, 0] for i in range(layers)], layer_of)
-    part = lane_vector([frac[0, i, 0].astype(F32) * (1.0 / 16.0) for i in range(layers)], layer_of)
-    offset = me * band + index - layer_of * band - first
-    delta = offset - iota((P_SIZE, layers * band), 0)
-    pick = jnp.where(delta == 0, 1.0 - part, jnp.where(delta == 1, part, 0.0)).astype(BF16)
     total = jnp.dot(pick, jnp.concatenate(high, 0), preferred_element_type=F32)
     total = total + jnp.dot(pick, jnp.concatenate(low, 0), preferred_element_type=F32)
     coded = jnp.floor(total * (65536.0 / 6.283185307179586) + 0.5).astype(I32)
@@ -91,38 +107,56 @@
     send[...] = jnp.where(odd, upper, lower).astype(I16)
 
 
-def dirichlet(steps, flip):
-    size = jnp.abs(steps)
-    near = jnp.minimum(size, PAD - size)
-    turns = near.astype(F32) * (0.5 / PAD)
-    sine = horner(SIN_TERMS, turns * turns) * turns
-    quarter = jnp.bitwise_and(steps, 3)
-    negative = (quarter == 3) != ((steps < 0) != flip)
-    value = 1.0 / (jnp.where(negative, -float(PAD), float(PAD)) * sine)
-    odd = jnp.bitwise_and(steps, 1) == 1
-    return jnp.where(odd, value, jnp.where(steps == 0, 0.5, 0.0)).astype(BF16)
-
-
 def shift_of(facet, quadrant, axis):
     side = quadrant // 2 if axis == 0 else quadrant % 2
-    return facet[quadrant, axis] * (2 * side - 1), side == 0
-
-
-def table_kernel(facet, left, right, *, rows, padded, lanes):
+    return facet[axis, quadrant] * (2 * side - 1), side == 0
+
+
+def half_band():
+    steps = np.arange(PAD + P_SIZE + 24)[:, None] - P_SIZE - np.arange(PAD)[None, :]
+    odd = (steps % 2 != 0) & (np.abs(steps) < PAD)
+    sine = np.sin(np.pi / PAD * np.where(odd, steps, 1))
+    value = np.where(odd, (2 - steps % 4) / (PAD * sine), np.where(steps == 0, 0.5, 0.0))
+    return value.astype(jnp.bfloat16).astype(np.float32)
+
+
+def window(band, start, count, width):
+    whole = lax.shift_right_logical(start, 3) * 8
+    block = band[pl.ds(pl.multiple_of(whole, 8), count + 8), :width]
+    return pltpu.roll(block, count + 8 - (start - whole), 0)[:count]
+
+
+def table_kernel(facet_hbm, band, own, left, right, turns, passed, facet, sem, *, rows, padded, lanes):
+    copy = pltpu.make_async_copy(facet_hbm, facet, sem)
+    copy.start()
+    passed[...] = own[...]
+    copy.wait()
     first = lax.axis_index("mod") * rows
+    signs = 1.0 - 2.0 * jnp.bitwise_and(iota((8, PAD), 0) + iota((8, PAD), 1), 1).astype(F32)
+    quad = iota((8, lanes), 0)
+    facet_steps = jnp.zeros((8, lanes), I32)
     for quadrant in range(4):
-        shift, flip = shift_of(facet, quadrant, 0)
-        steps = iota((padded, P_SIZE), 0) - iota((padded, P_SIZE), 1) + (first - HALF - shift)
-        left[pl.ds(quadrant * padded, padded), :] = dirichlet(steps, flip)
-        shift, flip = shift_of(facet, quadrant, 1)
-        source = iota((lanes, PAD), 0)
-        steps = iota((lanes, PAD), 1) - source + (-HALF - shift)
-        value = dirichlet(steps, flip)
-        right[pl.ds(quadrant * lanes, lanes), :] = jnp.where(source < P_SIZE, value, 0.0).astype(BF16)
+        row_shift, row_flip = shift_of(facet, quadrant, 0)
+        col_shift, col_flip = shift_of(facet, quadrant, 1)
+        start = first + HALF - row_shift
+        piece = window(band, start, padded, P_SIZE)
+        if row_flip:
+            flips = signs[:, :P_SIZE] * (1 - 2 * jnp.bitwise_and(start, 1)).astype(F32)
+            piece = piece * jnp.concatenate([flips] * (padded // 8), 0)
+        left[pl.ds(quadrant * padded, padded), :] = piece.astype(BF16)
+        start = col_shift + (HALF + P_SIZE)
+        piece = window(band, start, P_SIZE, PAD)
+        if col_flip:
+            flips = signs * (1 - 2 * jnp.bitwise_and(start, 1)).astype(F32)
+            piece = piece * jnp.concatenate([flips] * (P_SIZE // 8), 0)
+        right[pl.ds(quadrant * lanes, P_SIZE), :] = piece.astype(BF16)
+        right[pl.ds(quadrant * lanes + P_SIZE, lanes - P_SIZE), :] = jnp.zeros((lanes - P_SIZE, PAD), BF16)
+        facet_steps = jnp.where(quad == quadrant, (row_shift + col_shift) * (-2 * (PAD - 2)), facet_steps)
+    turns[...] = facet_steps
 
 
 def image_kernel(
-    facet, own, other, left, right, out, row_re, row_im, col_re, col_im, field_re, field_im, total, *, count, padded, lanes
+    facet_steps, own, other, left, right, out, row_re, row_im, col_re, col_im, field_re, field_im, total, *, count, padded, lanes
 ):
     me = lax.axis_index("mod")
     odd = lax.rem(me, 2) == 1
@@ -145,14 +179,9 @@
         place = P_SIZE - base + point
         row_re[point] = jnp.broadcast_to(cos_rows[:, place : place + 1], (P_SIZE, 128))
         row_im[point] = jnp.broadcast_to(sin_rows[:, place : place + 1], (P_SIZE, 128))
-    quad = iota((8, 1), 0)
-    facet_steps = jnp.zeros((8, 1), I32)
-    for quadrant in range(4):
-        shift = shift_of(facet, quadrant, 0)[0] + shift_of(facet, quadrant, 1)[0]
-        facet_steps = jnp.where(quad == quadrant, shift * (-2 * (PAD - 2)), facet_steps)
     for point in range(count):
         tilt_col = mine[point : point + 1, lanes - 1 : lanes]
-        steps = (tilt_col - CENTRE) * iota((8, lanes), 1) + facet_steps
+        steps = (tilt_col - CENTRE) * iota((8, lanes), 1) + facet_steps[...]
         turn_re, turn_im = cos_sin(centred(steps.astype(F32) * (1.0 / FINE)))
         col_re[point] = turn_re
         col_im[point] = turn_im
@@ -180,7 +209,7 @@
         total[...] += image_re * image_re + image_im * image_im
         return carry
 
-    lax.fori_loop(0, count, one_point, 0)
+    lax.fori_loop(0, count, one_point, 0, unroll=min(count, 8))
     out[0] = total[: out.shape[1]] * (4.0 / count)
 
 
@@ -195,40 +224,51 @@
     rows = PAD // peers
     padded = round_up(rows, 16)
     lanes = round_up(P_SIZE + count + 1, 128)
-    smem = pl.BlockSpec(memory_space=pltpu.SMEM)
+    hbm = pl.BlockSpec(memory_space=pltpu.HBM)
     vmem = pl.BlockSpec(memory_space=pltpu.VMEM)
     params = pltpu.CompilerParams(vmem_limit_bytes=40 * 1024 * 1024)
     half_shape = jax.ShapeDtypeStruct((HALF, lanes), I16)
     keep, send = pl.pallas_call(
         functools.partial(phase_kernel, lanes=lanes),
         out_shape=(half_shape, half_shape),
-        in_specs=[smem, smem, smem, vmem],
+        in_specs=[hbm, hbm, hbm, hbm],
         out_specs=(vmem, vmem),
-        compiler_params=params,
+        scratch_shapes=[
+            pltpu.SMEM((1, 2, layers), I32),
+            pltpu.SMEM((1, 2, layers), I32),
+            pltpu.SMEM(tilt_steps.shape, I32),
+            pltpu.VMEM(screens.shape, F32),
+            pltpu.SemaphoreType.DMA((3,)),
+            pltpu.SemaphoreType.DMA((layers,)),
+        ],
+        compiler_params=pltpu.CompilerParams(vmem_limit_bytes=60 * 1024 * 1024),
         name="phase_parts",
-    )(footprint, fraction, tilt_steps, screens)
-    left, right = pl.pallas_call(
+    )(footprint.swapaxes(1, 2), fraction.swapaxes(1, 2), tilt_steps, screens)
+    own = keep + swapped(send, peers, 1)
+    left, right, turns, passed = pl.pallas_call(
         functools.partial(table_kernel, rows=rows, padded=padded, lanes=lanes),
         out_shape=(
             jax.ShapeDtypeStruct((4 * padded, P_SIZE), BF16),
             jax.ShapeDtypeStruct((4 * lanes, PAD), BF16),
+            jax.ShapeDtypeStruct((8, lanes), I32),
+            half_shape,
         ),
-        in_specs=[smem],
-        out_specs=(vmem, vmem),
+        in_specs=[hbm, vmem, vmem],
+        out_specs=(vmem, vmem, vmem, vmem),
+        scratch_shapes=[pltpu.SMEM((2, 4), I32), pltpu.SemaphoreType.DMA(())],
         compiler_params=params,
-        cost_estimate=pl.CostEstimate(flops=30_000_000, bytes_accessed=2_500_000, transcendentals=0),
+        cost_estimate=pl.CostEstimate(flops=5_000_000_000, bytes_accessed=20_000_000, transcendentals=0),
         name="half_band_tables",
-    )(facet_shift)
-    own = keep + swapped(send, peers, 1)
+    )(facet_shift.T, jnp.asarray(half_band()), own)
     step = 2
     while step < peers:
-        own = own + swapped(own, peers, step)
+        own = passed = passed + swapped(own, peers, step)
         step *= 2
     other = swapped(own, peers, 1)
     return pl.pallas_call(
         functools.partial(image_kernel, count=count, padded=padded, lanes=lanes),
         out_shape=jax.ShapeDtypeStruct((1, rows, PAD), F32),
-        in_specs=[smem, vmem, vmem, vmem, vmem],
+        in_specs=[vmem, vmem, vmem, vmem, vmem],
         out_specs=vmem,
         scratch_shapes=[
             pltpu.VMEM((count, P_SIZE, 128), F32),
@@ -241,7 +281,7 @@
         ],
         compiler_params=params,
         name="detector_rows",
-    )(facet_shift, own, other, left, right)
+    )(turns, own, other, left, right)
 
 
 def solution(mesh):

time: 38.9 us -> 28.8 us (0.74)
  Pallas kernels: 26.2 us -> 19.2 us
  waiting for transfers between devices: 4.61 us -> 2.51 us
  local copies, waits for them, and re-layouts: 4.2 us -> 2.39 us
  other arithmetic: 0.07 us -> 0.97 us
    pallas_call x1, Pallas kernels: 18.7 us -> 13.6 us  [shards(): pl.pallas_call(functools.partial(image_kernel, count=count, padded=padded...]
    pallas_call x1, Pallas kernels: 5.83 us -> 2.37 us  [shards(): pl.pallas_call(functools.partial(table_kernel, rows=rows, padded=padded,...]
    ppermute x3, waiting for transfers between devices: 4.61 us -> 2.51 us  [swapped(): return lax.ppermute(values, 'mod', [(i, i ^ step) for i in range(peers)])]
    unnamed x7 -> x4, local copies, waits for them, and re-layouts: 4.2 us -> 2.39 us
    pallas_call x1, Pallas kernels: 1.69 us -> 3.25 us  [shards(): pl.pallas_call(functools.partial(phase_kernel, lanes=lanes), out_shape=(h...]
    add x1, other arithmetic: 0.03 us -> 0.94 us  [shards(): own = keep + swapped(send, peers, 1)]
  transfers between devices with their start and end apart: 3 -> 3, of which waited for: 2 -> 2; matrix products, arithmetic and copies ran while one was open for 2% -> 0% of each run, Pallas kernels for 15% -> 8%
where the time goes in v1:
time: 28.8 us; the launch traced here: 28.6 us
  Pallas kernels  19.2 us (67%)
  starting transfers between devices  3.53 us (12%)
  waiting for transfers between devices  2.51 us (9%)
  local copies, waits for them, and re-layouts  2.39 us (8%)
  other arithmetic  0.97 us (3%)
    pallas_call x1, Pallas kernels, shards(): pl.pallas_call(functools.partial(image_kernel, count=count, padded=padded...  13.6 us
    ppermute x3, starting transfers between devices, swapped(): return lax.ppermute(values, 'mod', [(i, i ^ step) for i in range(peers)])  3.53 us
    pallas_call x1, Pallas kernels, shards(): pl.pallas_call(functools.partial(phase_kernel, lanes=lanes), out_shape=(h...  3.25 us
    ppermute x3, waiting for transfers between devices, swapped(): return lax.ppermute(values, 'mod', [(i, i ^ step) for i in range(peers)])  2.51 us
    unnamed x4, local copies, waits for them, and re-layouts  2.39 us
    pallas_call x1, Pallas kernels, shards(): pl.pallas_call(functools.partial(table_kernel, rows=rows, padded=padded,...  2.37 us
    add x1, other arithmetic, shards(): own = keep + swapped(send, peers, 1)  0.94 us
  transfers between devices with their start and end apart: 3, of which 2 were waited for; matrix products, arithmetic and copies ran while one was open for 0% of the time, Pallas kernels for 8%

profile of v1, /device:TPU:0, one launch (start us, length us, event | category | flops | bytes accessed | tf_op | source)
XLA Modules:
  0.0 28.6 jit_solution(1143159195109160447)
XLA Ops:
  0.0 3.3 %phase_parts.1 = (s16[160,384]{1,0:T(8,128)(2,1)}, s16[160,384]{1,0:T(8,128)(2,1)}) custom-call(s32[1,2,4]{2,1,0:T(2,128)} %bitcast.4, s32[1,2,4]{2,1,0:T(2,128)} %bitcast.5, s32[2,2]{1,0:T(2,128)} %tilt_hbm.1, f32[4,128,512]{2,1,0:T(8,128)} %screens_hbm.1), custom_call_target="tpu_custom_call" | custom-call | tf_op jit(solution)/shard_map/phase_parts/pallas_call | solution.py:231
  3.3 0.5 %collective-permute-start = (s16[160,384]{1,0:T(8,128)(2,1)}, s16[160,384]{1,0:T(8,128)(2,1)S(1)}, u32[]{:S(2)}, u32[]{:S(2)}) collective-permute-start(s16[160,384]{1,0:T(8,128)(2,1)} %get-tuple-element.12), channel_id=1, source_target_pairs={{0,4},{4,0},{8,12},{12,8},{1,5},{5,1},{9,13},{13,9},{2,6},{6,2},{1... | collective-permute-start | bytes 368648 | tf_op jit(solution)/shard_map/ppermute | solution.py:217
  3.8 1.2 %collective-permute-done = s16[160,384]{1,0:T(8,128)(2,1)S(1)} collective-permute-done((s16[160,384]{1,0:T(8,128)(2,1)}, s16[160,384]{1,0:T(8,128)(2,1)S(1)}, u32[]{:S(2)}, u32[]{:S(2)}) %collective-permute-start) | collective-permute-done | bytes 122912 | tf_op jit(solution)/shard_map/ppermute | solution.py:217
  5.0 0.9 %add.6.own = s16[160,384]{1,0:T(8,128)(2,1)S(1)} add(s16[160,384]{1,0:T(8,128)(2,1)} %get-tuple-element.11, s16[160,384]{1,0:T(8,128)(2,1)S(1)} %collective-permute-done) | non-fusion elementwise | flops 61440 | bytes 368640 | tf_op jit(solution)/shard_map/add | solution.py:247
  5.9 2.9 %collective-permute-start.1 = (s16[160,384]{1,0:T(8,128)(2,1)S(1)}, s16[160,384]{1,0:T(8,128)(2,1)S(1)}, u32[]{:S(2)}, u32[]{:S(2)}) collective-permute-start(s16[160,384]{1,0:T(8,128)(2,1)S(1)} %add.6.own), channel_id=1, source_target_pairs={{0,8},{4,12},{8,0},{12,4},{1,9},{5,13},{9,1},{13,5},{2,10},{6,14},... | collective-permute-start | bytes 368648 | tf_op jit(solution)/shard_map/ppermute | solution.py:217
  8.9 0.0 copy-start
  8.9 0.7 %copy-done = s32[4,2]{0,1:T(2,128)S(1)} copy-done((s32[4,2]{0,1:T(2,128)S(1)}, s32[4,2]{0,1:T(2,128)}, u32[]{:S(2)}) %copy-start) | copy-done | bytes 56
  9.5 0.0 copy-start.1
  9.5 1.7 %copy-done.1 = f32[984,640]{1,0:T(8,128)S(1)} copy-done((f32[984,640]{1,0:T(8,128)S(1)}, f32[984,640]{1,0:T(8,128)}, u32[]{:S(2)}) %copy-start.1) | copy-done | bytes 2519064
  11.2 2.4 %half_band_tables.1 = (bf16[640,320]{1,0:T(8,128)(2,1)S(1)}, bf16[1536,640]{1,0:T(8,128)(2,1)S(1)}, s32[8,384]{1,0:T(8,128)S(1)}, s16[160,384]{1,0:T(8,128)(2,1)S(1)}) custom-call(s32[2,4]{1,0:T(2,128)S(1)} %bitcast.3, f32[984,640]{1,0:T(8,128)S(1)} %copy-done.1, s16[160,384]{1,0:T(8,128)(2,1)S(1)} %add.6.own), custom_call_target="tpu_custom_call" | custom-call | flops 5000000000 | bytes 20000000 | tf_op jit(solution)/shard_map/half_band_tables/pallas_call | solution.py:248
  13.6 0.0 collective-permute-done.1
  13.7 0.1 collective-permute-start.2
  13.8 1.3 %collective-permute-done.2.other = s16[160,384]{1,0:T(8,128)(2,1)S(1)} collective-permute-done((s16[160,384]{1,0:T(8,128)(2,1)S(1)}, s16[160,384]{1,0:T(8,128)(2,1)S(1)}, u32[]{:S(2)}, u32[]{:S(2)}) %collective-permute-start.2) | collective-permute-done | bytes 122912 | tf_op jit(solution)/shard_map/ppermute | solution.py:217
  15.1 13.6 %detector_rows.1 = f32[1,160,640]{2,1,0:T(8,128)} custom-call(s32[8,384]{1,0:T(8,128)S(1)} %get-tuple-element.13.facet_steps, s16[160,384]{1,0:T(8,128)(2,1)S(1)} %add.7.own, s16[160,384]{1,0:T(8,128)(2,1)S(1)} %collective-permute-done.2.other, bf16[640,320]{1,0:T(8,128)(2,1)S(1)} %get-tuple-element.15.left, bf16[1536,640]{1,0:T(8,128)(2,1)S(1)} %get-tuple-element.16.right), custom_call_target="tpu_custom_call" | custom-call | tf_op jit(solution)/shard_map/detector_rows/pallas_call | solution.py:268
  (1 shorter events, 0.0 us)
Async XLA Ops:
  3.3 1.7 %collective-permute-start = (s16[160,384]{1,0:T(8,128)(2,1)}, s16[160,384]{1,0:T(8,128)(2,1)S(1)}, u32[]{:S(2)}, u32[]{:S(2)}) collective-permute-start(s16[160,384]{1,0:T(8,128)(2,1)} %get-tuple-element.12), channel_id=1, source_target_pairs={{0,4},{4,0},{8,12},{12,8},{1,5},{5,1},{9,13},{13,9},{2,6},{6,2},{1... | collective-permute-start | bytes 368648 | tf_op jit(solution)/shard_map/ppermute | solution.py:217
  5.9 7.7 %collective-permute-start.1 = (s16[160,384]{1,0:T(8,128)(2,1)S(1)}, s16[160,384]{1,0:T(8,128)(2,1)S(1)}, u32[]{:S(2)}, u32[]{:S(2)}) collective-permute-start(s16[160,384]{1,0:T(8,128)(2,1)S(1)} %add.6.own), channel_id=1, source_target_pairs={{0,8},{4,12},{8,0},{12,4},{1,9},{5,13},{9,1},{13,5},{2,10},{6,14},... | collective-permute-start | bytes 368648 | tf_op jit(solution)/shard_map/ppermute | solution.py:217
  8.9 0.7 %copy-start = (s32[4,2]{0,1:T(2,128)S(1)}, s32[4,2]{0,1:T(2,128)}, u32[]{:S(2)}) copy-start(s32[4,2]{0,1:T(2,128)} %param.10) | copy-start | bytes 100
  9.5 1.7 %copy-start.1 = (f32[984,640]{1,0:T(8,128)S(1)}, f32[984,640]{1,0:T(8,128)}, u32[]{:S(2)}) copy-start(f32[984,640]{1,0:T(8,128)} %constant.2.clone.band) | copy-start | bytes 7557124
  13.7 1.4 %collective-permute-start.2 = (s16[160,384]{1,0:T(8,128)(2,1)S(1)}, s16[160,384]{1,0:T(8,128)(2,1)S(1)}, u32[]{:S(2)}, u32[]{:S(2)}) collective-permute-start(s16[160,384]{1,0:T(8,128)(2,1)S(1)} %add.7.own), channel_id=1, source_target_pairs={{0,4},{4,0},{8,12},{12,8},{1,5},{5,1},{9,13},{13,9},{2,6},{6,2},{1... | collective-permute-start | bytes 368648 | tf_op jit(solution)/shard_map/ppermute | solution.py:217

commit v2 on v1

--- a/solution.py
+++ b/solution.py
@@ -1,8 +1,8 @@
 import functools
+import math
 
 import jax
 import jax.numpy as jnp
-import numpy as np
 from jax import lax
 from jax.experimental import pallas as pl
 from jax.experimental.pallas import tpu as pltpu
@@ -112,51 +112,60 @@
     return facet[axis, quadrant] * (2 * side - 1), side == 0
 
 
-def half_band():
-    steps = np.arange(PAD + P_SIZE + 24)[:, None] - P_SIZE - np.arange(PAD)[None, :]
-    odd = (steps % 2 != 0) & (np.abs(steps) < PAD)
-    sine = np.sin(np.pi / PAD * np.where(odd, steps, 1))
-    value = np.where(odd, (2 - steps % 4) / (PAD * sine), np.where(steps == 0, 0.5, 0.0))
-    return value.astype(jnp.bfloat16).astype(np.float32)
-
-
-def window(band, start, count, width):
-    whole = lax.shift_right_logical(start, 3) * 8
-    block = band[pl.ds(pl.multiple_of(whole, 8), count + 8), :width]
-    return pltpu.roll(block, count + 8 - (start - whole), 0)[:count]
-
-
-def table_kernel(facet_hbm, band, own, left, right, turns, passed, facet, sem, *, rows, padded, lanes):
+def dirichlet(steps, flip):
+    size = jnp.abs(steps)
+    near = jnp.minimum(size, PAD - size)
+    turns = near.astype(F32) * (0.5 / PAD)
+    sine = horner(SIN_TERMS, turns * turns) * turns
+    negative = ((jnp.bitwise_and(steps, 3) == 3) != (steps < 0)) != flip
+    value = 1.0 / (jnp.where(negative, -float(PAD), float(PAD)) * sine)
+    odd = jnp.bitwise_and(steps, 1) == 1
+    return jnp.where(odd, value, jnp.where(steps == 0, 0.5, 0.0))
+
+
+def toeplitz(top, flip, rows, width):
+    lane = iota((8, width), 1)
+    lane = jnp.where(lane >= width - rows, lane - width, lane)
+    first = dirichlet(top - lane, flip)
+    return pltpu.roll(jnp.concatenate([first] * (rows // 8), 0), 0, 1, stride=1, stride_axis=0)
+
+
+def table_kernel(facet_hbm, own, left, right, turns, passed, facet, sem, *, rows, padded, lanes):
     copy = pltpu.make_async_copy(facet_hbm, facet, sem)
     copy.start()
     passed[...] = own[...]
     copy.wait()
     first = lax.axis_index("mod") * rows
-    signs = 1.0 - 2.0 * jnp.bitwise_and(iota((8, PAD), 0) + iota((8, PAD), 1), 1).astype(F32)
     quad = iota((8, lanes), 0)
     facet_steps = jnp.zeros((8, lanes), I32)
+    blocks = PAD // 128
+    spill = P_SIZE % 128
+    whole = P_SIZE // 128
+    narrow = round_up(P_SIZE + padded, 128)
+    wide = (2 * blocks - 1) * 128
     for quadrant in range(4):
         row_shift, row_flip = shift_of(facet, quadrant, 0)
         col_shift, col_flip = shift_of(facet, quadrant, 1)
-        start = first + HALF - row_shift
-        piece = window(band, start, padded, P_SIZE)
-        if row_flip:
-            flips = signs[:, :P_SIZE] * (1 - 2 * jnp.bitwise_and(start, 1)).astype(F32)
-            piece = piece * jnp.concatenate([flips] * (padded // 8), 0)
-        left[pl.ds(quadrant * padded, padded), :] = piece.astype(BF16)
-        start = col_shift + (HALF + P_SIZE)
-        piece = window(band, start, P_SIZE, PAD)
-        if col_flip:
-            flips = signs * (1 - 2 * jnp.bitwise_and(start, 1)).astype(F32)
-            piece = piece * jnp.concatenate([flips] * (P_SIZE // 8), 0)
-        right[pl.ds(quadrant * lanes, P_SIZE), :] = piece.astype(BF16)
-        right[pl.ds(quadrant * lanes + P_SIZE, lanes - P_SIZE), :] = jnp.zeros((lanes - P_SIZE, PAD), BF16)
+        piece = toeplitz(first - HALF - row_shift, row_flip, padded, narrow)
+        left[pl.ds(quadrant * padded, padded), :] = piece[:, :P_SIZE].astype(BF16)
         facet_steps = jnp.where(quad == quadrant, (row_shift + col_shift) * (-2 * (PAD - 2)), facet_steps)
     turns[...] = facet_steps
+    lane = iota((128, 128), 1)
+    for pair in range(2):
+        pieces = []
+        for side in range(2):
+            col_shift, col_flip = shift_of(facet, 2 * pair + side, 1)
+            top = (blocks - 1) * 128 + side * spill - HALF - col_shift
+            pieces.append(toeplitz(top, col_flip, 128, wide))
+        for block in range(blocks):
+            even, odd = (piece[:, (blocks - 1 - block) * 128 :] for piece in pieces)
+            edge = jnp.where(lane < spill, even[:, whole * 128 : whole * 128 + 128], odd[:, :128])
+            joined = [even[:, : whole * 128], edge, odd[:, 128 : whole * 128 + 128]]
+            right[pl.ds(block * 128, 128), pl.ds(pair * 2 * P_SIZE, 2 * P_SIZE)] = jnp.concatenate(joined, 1).astype(BF16)
 
 
 def image_kernel(
-    facet_steps, own, other, left, right, out, row_re, row_im, col_re, col_im, field_re, field_im, total, *, count, padded, lanes
+    facet_steps, own, other, left, right, out, row_re, row_im, col_re, col_im, field_re, field_im, total, *, count, group, padded, lanes
 ):
     me = lax.axis_index("mod")
     odd = lax.rem(me, 2) == 1
@@ -187,30 +196,37 @@
         col_im[point] = turn_im
     total[...] = jnp.zeros_like(total)
 
-    def one_point(point, carry):
+    def one_group(index, carry):
         copies = lanes // 128
-        turn_re = jnp.concatenate([row_re[point]] * copies, 1)
-        turn_im = jnp.concatenate([row_im[point]] * copies, 1)
-        wide_re, wide_im = field_re[...], field_im[...]
-        moved_re = (wide_re * turn_re - wide_im * turn_im).astype(BF16)
-        moved_im = (wide_re * turn_im + wide_im * turn_re).astype(BF16)
-        half = jnp.dot(left[...], jnp.concatenate([moved_re, moved_im], 1), preferred_element_type=F32)
-        parts_re, parts_im = [], []
-        for quadrant in range(4):
-            piece = half[quadrant * padded : (quadrant + 1) * padded]
-            piece_re, piece_im = piece[:, :lanes], piece[:, lanes:]
-            turn_re = col_re[point, quadrant : quadrant + 1, :]
-            turn_im = col_im[point, quadrant : quadrant + 1, :]
-            parts_re.append((piece_re * turn_re - piece_im * turn_im).astype(BF16))
-            parts_im.append((piece_re * turn_im + piece_im * turn_re).astype(BF16))
-        stacked = jnp.concatenate([jnp.concatenate(parts_re, 1), jnp.concatenate(parts_im, 1)], 0)
-        image = jnp.dot(stacked, right[...], preferred_element_type=F32)
-        image_re, image_im = image[:padded], image[padded:]
-        total[...] += image_re * image_re + image_im * image_im
+        stacked = []
+        for member in range(group):
+            point = index * group + member
+            turn_re = jnp.concatenate([row_re[point]] * copies, 1)
+            turn_im = jnp.concatenate([row_im[point]] * copies, 1)
+            wide_re, wide_im = field_re[...], field_im[...]
+            moved_re = (wide_re * turn_re - wide_im * turn_im).astype(BF16)
+            moved_im = (wide_re * turn_im + wide_im * turn_re).astype(BF16)
+            half = jnp.dot(left[...], jnp.concatenate([moved_re, moved_im], 1), preferred_element_type=F32)
+            parts_re, parts_im = [], []
+            for quadrant in range(4):
+                piece = half[quadrant * padded : (quadrant + 1) * padded]
+                piece_re, piece_im = piece[:, :lanes], piece[:, lanes:]
+                turn_re = col_re[point, quadrant : quadrant + 1, :]
+                turn_im = col_im[point, quadrant : quadrant + 1, :]
+                parts_re.append((piece_re * turn_re - piece_im * turn_im).astype(BF16)[:, :P_SIZE])
+                parts_im.append((piece_re * turn_im + piece_im * turn_re).astype(BF16)[:, :P_SIZE])
+            stacked += [jnp.concatenate(parts_re, 1), jnp.concatenate(parts_im, 1)]
+        image = lax.dot_general(
+            right[...], jnp.concatenate(stacked, 0), (((1,), (1,)), ((), ())), preferred_element_type=F32
+        )
+        total[...] += image * image
         return carry
 
-    lax.fori_loop(0, count, one_point, 0, unroll=min(count, 8))
-    out[0] = total[: out.shape[1]] * (4.0 / count)
+    lax.fori_loop(0, count // group, one_group, 0, unroll=min(count // group, 2))
+    folded = total[:, :padded]
+    for block in range(1, 2 * group):
+        folded = folded + total[:, block * padded : (block + 1) * padded]
+    out[0] = folded.T[: out.shape[1]] * (4.0 / count)
 
 
 def swapped(values, peers, step):
@@ -221,6 +237,7 @@
     peers = lax.axis_size("mod")
     layers, band, width = screens.shape
     count = tilt_steps.shape[0] * peers
+    group = math.gcd(count, 4)
     rows = PAD // peers
     padded = round_up(rows, 16)
     lanes = round_up(P_SIZE + count + 1, 128)
@@ -249,24 +266,24 @@
         functools.partial(table_kernel, rows=rows, padded=padded, lanes=lanes),
         out_shape=(
             jax.ShapeDtypeStruct((4 * padded, P_SIZE), BF16),
-            jax.ShapeDtypeStruct((4 * lanes, PAD), BF16),
+            jax.ShapeDtypeStruct((PAD, 4 * P_SIZE), BF16),
             jax.ShapeDtypeStruct((8, lanes), I32),
             half_shape,
         ),
-        in_specs=[hbm, vmem, vmem],
+        in_specs=[hbm, vmem],
         out_specs=(vmem, vmem, vmem, vmem),
         scratch_shapes=[pltpu.SMEM((2, 4), I32), pltpu.SemaphoreType.DMA(())],
         compiler_params=params,
         cost_estimate=pl.CostEstimate(flops=5_000_000_000, bytes_accessed=20_000_000, transcendentals=0),
         name="half_band_tables",
-    )(facet_shift.T, jnp.asarray(half_band()), own)
+    )(facet_shift.T, own)
     step = 2
     while step < peers:
         own = passed = passed + swapped(own, peers, step)
         step *= 2
     other = swapped(own, peers, 1)
     return pl.pallas_call(
-        functools.partial(image_kernel, count=count, padded=padded, lanes=lanes),
+        functools.partial(image_kernel, count=count, group=group, padded=padded, lanes=lanes),
         out_shape=jax.ShapeDtypeStruct((1, rows, PAD), F32),
         in_specs=[vmem, vmem, vmem, vmem, vmem],
         out_specs=vmem,
@@ -277,7 +294,7 @@
             pltpu.VMEM((count, 8, lanes), F32),
             pltpu.VMEM((P_SIZE, lanes), F32),
             pltpu.VMEM((P_SIZE, lanes), F32),
-            pltpu.VMEM((padded, PAD), F32),
+            pltpu.VMEM((PAD, 2 * group * padded), F32),
         ],
         compiler_params=params,
         name="detector_rows",

time: 28.8 us -> 25.8 us (0.90)
  Pallas kernels: 19.2 us -> 16.2 us
  waiting for transfers between devices: 2.51 us -> 4.29 us
  local copies, waits for them, and re-layouts: 2.39 us -> 0.68 us
    pallas_call x1, Pallas kernels: 13.6 us -> 11.8 us  [shards(): pl.pallas_call(functools.partial(image_kernel, count=count, group=group,...]
    ppermute x3, waiting for transfers between devices: 2.51 us -> 4.29 us  [swapped(): return lax.ppermute(values, 'mod', [(i, i ^ step) for i in range(peers)])]
    unnamed x4 -> x2, local copies, waits for them, and re-layouts: 2.39 us -> 0.68 us
    pallas_call x1, Pallas kernels: 2.37 us -> 1.17 us  [shards(): pl.pallas_call(functools.partial(table_kernel, rows=rows, padded=padded,...]
  transfers between devices with their start and end apart: 3 -> 3, of which waited for: 2 -> 3; matrix products, arithmetic and copies ran while one was open for 0% -> 0% of each run, Pallas kernels for 8% -> 5%
where the time goes in v2:
time: 25.8 us; the launch traced here: 25.7 us
  Pallas kernels  16.2 us (63%)
  waiting for transfers between devices  4.29 us (17%)
  starting transfers between devices  3.53 us (14%)
  other arithmetic  0.97 us (4%)
  local copies, waits for them, and re-layouts  0.68 us (3%)
    pallas_call x1, Pallas kernels, shards(): pl.pallas_call(functools.partial(image_kernel, count=count, group=group,...  11.8 us
    ppermute x3, waiting for transfers between devices, swapped(): return lax.ppermute(values, 'mod', [(i, i ^ step) for i in range(peers)])  4.29 us
    ppermute x3, starting transfers between devices, swapped(): return lax.ppermute(values, 'mod', [(i, i ^ step) for i in range(peers)])  3.53 us
    pallas_call x1, Pallas kernels, shards(): pl.pallas_call(functools.partial(phase_kernel, lanes=lanes), out_shape=(h...  3.25 us
    pallas_call x1, Pallas kernels, shards(): pl.pallas_call(functools.partial(table_kernel, rows=rows, padded=padded,...  1.17 us
    add x1, other arithmetic, shards(): own = keep + swapped(send, peers, 1)  0.94 us
    unnamed x2, local copies, waits for them, and re-layouts  0.68 us
  transfers between devices with their start and end apart: 3, of which 3 were waited for; matrix products, arithmetic and copies ran while one was open for 0% of the time, Pallas kernels for 5%

profile of v2, /device:TPU:0, one launch (start us, length us, event | category | flops | bytes accessed | tf_op | source)
XLA Modules:
  0.0 25.7 jit_solution(9247561742729572676)
XLA Ops:
  0.0 3.3 %phase_parts.1 = (s16[160,384]{1,0:T(8,128)(2,1)}, s16[160,384]{1,0:T(8,128)(2,1)}) custom-call(s32[1,2,4]{2,1,0:T(2,128)} %bitcast.4, s32[1,2,4]{2,1,0:T(2,128)} %bitcast.5, s32[2,2]{1,0:T(2,128)} %tilt_hbm.1, f32[4,128,512]{2,1,0:T(8,128)} %screens_hbm.1), custom_call_target="tpu_custom_call" | custom-call | tf_op jit(solution)/shard_map/phase_parts/pallas_call | solution.py:248
  3.3 0.5 %collective-permute-start = (s16[160,384]{1,0:T(8,128)(2,1)}, s16[160,384]{1,0:T(8,128)(2,1)S(1)}, u32[]{:S(2)}, u32[]{:S(2)}) collective-permute-start(s16[160,384]{1,0:T(8,128)(2,1)} %get-tuple-element.12), channel_id=1, source_target_pairs={{0,4},{4,0},{8,12},{12,8},{1,5},{5,1},{9,13},{13,9},{2,6},{6,2},{1... | collective-permute-start | bytes 368648 | tf_op jit(solution)/shard_map/ppermute | solution.py:233
  3.8 1.2 %collective-permute-done = s16[160,384]{1,0:T(8,128)(2,1)S(1)} collective-permute-done((s16[160,384]{1,0:T(8,128)(2,1)}, s16[160,384]{1,0:T(8,128)(2,1)S(1)}, u32[]{:S(2)}, u32[]{:S(2)}) %collective-permute-start) | collective-permute-done | bytes 122912 | tf_op jit(solution)/shard_map/ppermute | solution.py:233
  5.0 0.9 %add.6.own = s16[160,384]{1,0:T(8,128)(2,1)S(1)} add(s16[160,384]{1,0:T(8,128)(2,1)} %get-tuple-element.11, s16[160,384]{1,0:T(8,128)(2,1)S(1)} %collective-permute-done) | non-fusion elementwise | flops 61440 | bytes 368640 | tf_op jit(solution)/shard_map/add | solution.py:264
  5.9 2.9 %collective-permute-start.1 = (s16[160,384]{1,0:T(8,128)(2,1)S(1)}, s16[160,384]{1,0:T(8,128)(2,1)S(1)}, u32[]{:S(2)}, u32[]{:S(2)}) collective-permute-start(s16[160,384]{1,0:T(8,128)(2,1)S(1)} %add.6.own), channel_id=1, source_target_pairs={{0,8},{4,12},{8,0},{12,4},{1,9},{5,13},{9,1},{13,5},{2,10},{6,14},... | collective-permute-start | bytes 368648 | tf_op jit(solution)/shard_map/ppermute | solution.py:233
  8.8 0.0 copy-start
  8.9 0.7 %copy-done = s32[4,2]{0,1:T(2,128)S(1)} copy-done((s32[4,2]{0,1:T(2,128)S(1)}, s32[4,2]{0,1:T(2,128)}, u32[]{:S(2)}) %copy-start) | copy-done | bytes 56
  9.5 1.2 %half_band_tables.1 = (bf16[640,320]{1,0:T(8,128)(2,1)S(1)}, bf16[640,1280]{1,0:T(8,128)(2,1)S(1)}, s32[8,384]{1,0:T(8,128)S(1)}, s16[160,384]{1,0:T(8,128)(2,1)S(1)}) custom-call(s32[2,4]{1,0:T(2,128)S(1)} %bitcast.3, s16[160,384]{1,0:T(8,128)(2,1)S(1)} %add.6.own), custom_call_target="tpu_custom_call" | custom-call | flops 5000000000 | bytes 20000000 | tf_op jit(solution)/shard_map/half_band_tables/pallas_call | solution.py:265
  10.7 1.8 %collective-permute-done.1 = s16[160,384]{1,0:T(8,128)(2,1)S(1)} collective-permute-done((s16[160,384]{1,0:T(8,128)(2,1)S(1)}, s16[160,384]{1,0:T(8,128)(2,1)S(1)}, u32[]{:S(2)}, u32[]{:S(2)}) %collective-permute-start.1) | collective-permute-done | bytes 122912 | tf_op jit(solution)/shard_map/ppermute | solution.py:233
  12.5 0.1 collective-permute-start.2
  12.6 1.3 %collective-permute-done.2.other = s16[160,384]{1,0:T(8,128)(2,1)S(1)} collective-permute-done((s16[160,384]{1,0:T(8,128)(2,1)S(1)}, s16[160,384]{1,0:T(8,128)(2,1)S(1)}, u32[]{:S(2)}, u32[]{:S(2)}) %collective-permute-start.2) | collective-permute-done | bytes 122912 | tf_op jit(solution)/shard_map/ppermute | solution.py:233
  13.9 11.8 %detector_rows.1 = f32[1,160,640]{2,1,0:T(8,128)} custom-call(s32[8,384]{1,0:T(8,128)S(1)} %get-tuple-element.13.facet_steps, s16[160,384]{1,0:T(8,128)(2,1)S(1)} %add.7.own, s16[160,384]{1,0:T(8,128)(2,1)S(1)} %collective-permute-done.2.other, bf16[640,320]{1,0:T(8,128)(2,1)S(1)} %get-tuple-element.15.left, bf16[640,1280]{1,0:T(8,128)(2,1)S(1)} %get-tuple-element.16.right), custom_call_target="tpu_custom_call" | custom-call | tf_op jit(solution)/shard_map/detector_rows/pallas_call | solution.py:285
  (1 shorter events, 0.0 us)
Async XLA Ops:
  3.3 1.7 %collective-permute-start = (s16[160,384]{1,0:T(8,128)(2,1)}, s16[160,384]{1,0:T(8,128)(2,1)S(1)}, u32[]{:S(2)}, u32[]{:S(2)}) collective-permute-start(s16[160,384]{1,0:T(8,128)(2,1)} %get-tuple-element.12), channel_id=1, source_target_pairs={{0,4},{4,0},{8,12},{12,8},{1,5},{5,1},{9,13},{13,9},{2,6},{6,2},{1... | collective-permute-start | bytes 368648 | tf_op jit(solution)/shard_map/ppermute | solution.py:233
  5.9 6.6 %collective-permute-start.1 = (s16[160,384]{1,0:T(8,128)(2,1)S(1)}, s16[160,384]{1,0:T(8,128)(2,1)S(1)}, u32[]{:S(2)}, u32[]{:S(2)}) collective-permute-start(s16[160,384]{1,0:T(8,128)(2,1)S(1)} %add.6.own), channel_id=1, source_target_pairs={{0,8},{4,12},{8,0},{12,4},{1,9},{5,13},{9,1},{13,5},{2,10},{6,14},... | collective-permute-start | bytes 368648 | tf_op jit(solution)/shard_map/ppermute | solution.py:233
  8.8 0.7 %copy-start = (s32[4,2]{0,1:T(2,128)S(1)}, s32[4,2]{0,1:T(2,128)}, u32[]{:S(2)}) copy-start(s32[4,2]{0,1:T(2,128)} %param.9) | copy-start | bytes 100
  12.5 1.4 %collective-permute-start.2 = (s16[160,384]{1,0:T(8,128)(2,1)S(1)}, s16[160,384]{1,0:T(8,128)(2,1)S(1)}, u32[]{:S(2)}, u32[]{:S(2)}) collective-permute-start(s16[160,384]{1,0:T(8,128)(2,1)S(1)} %add.7.own), channel_id=1, source_target_pairs={{0,4},{4,0},{8,12},{12,8},{1,5},{5,1},{9,13},{13,9},{2,6},{6,2},{1... | collective-permute-start | bytes 368648 | tf_op jit(solution)/shard_map/ppermute | solution.py:233

commit v3 on v2

--- a/solution.py
+++ b/solution.py
@@ -247,7 +247,7 @@
     half_shape = jax.ShapeDtypeStruct((HALF, lanes), I16)
     keep, send = pl.pallas_call(
         functools.partial(phase_kernel, lanes=lanes),
-        out_shape=(half_shape, half_shape),
+        out_shape=(pltpu.VMEM((HALF, lanes), I16), pltpu.VMEM((HALF, lanes), I16)),
         in_specs=[hbm, hbm, hbm, hbm],
         out_specs=(vmem, vmem),
         scratch_shapes=[

time: 25.8 us -> 24 us (0.930)
  other arithmetic: 0.97 us -> 0.07 us
  Pallas kernels: 16.2 us -> 15.5 us
    add x1, other arithmetic: 0.94 us -> 0.03 us  [shards(): own = keep + swapped(send, peers, 1)]
    pallas_call x1, Pallas kernels: 3.25 us -> 2.57 us  [shards(): pl.pallas_call(functools.partial(phase_kernel, lanes=lanes), out_shape=(p...]
where the time goes in v3:
time: 24 us; the launch traced here: 23.9 us
  Pallas kernels  15.5 us (65%)
  waiting for transfers between devices  4.07 us (17%)
  starting transfers between devices  3.53 us (15%)
  local copies, waits for them, and re-layouts  0.68 us (3%)
    pallas_call x1, Pallas kernels, shards(): pl.pallas_call(functools.partial(image_kernel, count=count, group=group,...  11.7 us
    ppermute x3, waiting for transfers between devices, swapped(): return lax.ppermute(values, 'mod', [(i, i ^ step) for i in range(peers)])  4.07 us
    ppermute x3, starting transfers between devices, swapped(): return lax.ppermute(values, 'mod', [(i, i ^ step) for i in range(peers)])  3.53 us
    pallas_call x1, Pallas kernels, shards(): pl.pallas_call(functools.partial(phase_kernel, lanes=lanes), out_shape=(p...  2.57 us
    pallas_call x1, Pallas kernels, shards(): pl.pallas_call(functools.partial(table_kernel, rows=rows, padded=padded,...  1.17 us
    unnamed x2, local copies, waits for them, and re-layouts  0.68 us
  transfers between devices with their start and end apart: 3, of which 3 were waited for; matrix products, arithmetic and copies ran while one was open for 0% of the time, Pallas kernels for 5%

profile of v3, /device:TPU:0, one launch (start us, length us, event | category | flops | bytes accessed | tf_op | source)
XLA Modules:
  0.0 23.9 jit_solution(7006733245934476507)
XLA Ops:
  0.0 2.6 %phase_parts.1 = (s16[160,384]{1,0:T(8,128)(2,1)S(1)}, s16[160,384]{1,0:T(8,128)(2,1)S(1)}) custom-call(s32[1,2,4]{2,1,0:T(2,128)} %bitcast.4, s32[1,2,4]{2,1,0:T(2,128)} %bitcast.5, s32[2,2]{1,0:T(2,128)} %tilt_hbm.1, f32[4,128,512]{2,1,0:T(8,128)} %screens_hbm.1), custom_call_target="tpu_custom_call" | custom-call | tf_op jit(solution)/shard_map/phase_parts/pallas_call | solution.py:248
  2.6 0.5 %collective-permute-start = (s16[160,384]{1,0:T(8,128)(2,1)S(1)}, s16[160,384]{1,0:T(8,128)(2,1)S(1)}, u32[]{:S(2)}, u32[]{:S(2)}) collective-permute-start(s16[160,384]{1,0:T(8,128)(2,1)S(1)} %get-tuple-element.12), channel_id=1, source_target_pairs={{0,4},{4,0},{8,12},{12,8},{1,5},{5,1},{9,13},{13,9},{2,6},{6,2},{1... | collective-permute-start | bytes 368648 | tf_op jit(solution)/shard_map/ppermute | solution.py:233
  3.1 1.0 %collective-permute-done = s16[160,384]{1,0:T(8,128)(2,1)S(1)} collective-permute-done((s16[160,384]{1,0:T(8,128)(2,1)S(1)}, s16[160,384]{1,0:T(8,128)(2,1)S(1)}, u32[]{:S(2)}, u32[]{:S(2)}) %collective-permute-start) | collective-permute-done | bytes 122912 | tf_op jit(solution)/shard_map/ppermute | solution.py:233
  4.1 2.9 %collective-permute-start.1 = (s16[160,384]{1,0:T(8,128)(2,1)S(1)}, s16[160,384]{1,0:T(8,128)(2,1)S(1)}, u32[]{:S(2)}, u32[]{:S(2)}) collective-permute-start(s16[160,384]{1,0:T(8,128)(2,1)S(1)} %add.6.own), channel_id=1, source_target_pairs={{0,8},{4,12},{8,0},{12,4},{1,9},{5,13},{9,1},{13,5},{2,10},{6,14},... | collective-permute-start | bytes 368648 | tf_op jit(solution)/shard_map/ppermute | solution.py:233
  7.0 0.0 copy-start
  7.0 0.7 %copy-done = s32[4,2]{0,1:T(2,128)S(1)} copy-done((s32[4,2]{0,1:T(2,128)S(1)}, s32[4,2]{0,1:T(2,128)}, u32[]{:S(2)}) %copy-start) | copy-done | bytes 56
  7.7 1.2 %half_band_tables.1 = (bf16[640,320]{1,0:T(8,128)(2,1)S(1)}, bf16[640,1280]{1,0:T(8,128)(2,1)S(1)}, s32[8,384]{1,0:T(8,128)S(1)}, s16[160,384]{1,0:T(8,128)(2,1)S(1)}) custom-call(s32[2,4]{1,0:T(2,128)S(1)} %bitcast.3, s16[160,384]{1,0:T(8,128)(2,1)S(1)} %add.6.own), custom_call_target="tpu_custom_call" | custom-call | flops 5000000000 | bytes 20000000 | tf_op jit(solution)/shard_map/half_band_tables/pallas_call | solution.py:265
  8.9 1.8 %collective-permute-done.1 = s16[160,384]{1,0:T(8,128)(2,1)S(1)} collective-permute-done((s16[160,384]{1,0:T(8,128)(2,1)S(1)}, s16[160,384]{1,0:T(8,128)(2,1)S(1)}, u32[]{:S(2)}, u32[]{:S(2)}) %collective-permute-start.1) | collective-permute-done | bytes 122912 | tf_op jit(solution)/shard_map/ppermute | solution.py:233
  10.7 0.1 collective-permute-start.2
  10.8 1.3 %collective-permute-done.2.other = s16[160,384]{1,0:T(8,128)(2,1)S(1)} collective-permute-done((s16[160,384]{1,0:T(8,128)(2,1)S(1)}, s16[160,384]{1,0:T(8,128)(2,1)S(1)}, u32[]{:S(2)}, u32[]{:S(2)}) %collective-permute-start.2) | collective-permute-done | bytes 122912 | tf_op jit(solution)/shard_map/ppermute | solution.py:233
  12.1 11.7 %detector_rows.1 = f32[1,160,640]{2,1,0:T(8,128)} custom-call(s32[8,384]{1,0:T(8,128)S(1)} %get-tuple-element.13.facet_steps, s16[160,384]{1,0:T(8,128)(2,1)S(1)} %add.7.own, s16[160,384]{1,0:T(8,128)(2,1)S(1)} %collective-permute-done.2.other, bf16[640,320]{1,0:T(8,128)(2,1)S(1)} %get-tuple-element.15.left, bf16[640,1280]{1,0:T(8,128)(2,1)S(1)} %get-tuple-element.16.right), custom_call_target="tpu_custom_call" | custom-call | tf_op jit(solution)/shard_map/detector_rows/pallas_call | solution.py:285
  (2 shorter events, 0.1 us)
Async XLA Ops:
  2.6 1.5 %collective-permute-start = (s16[160,384]{1,0:T(8,128)(2,1)S(1)}, s16[160,384]{1,0:T(8,128)(2,1)S(1)}, u32[]{:S(2)}, u32[]{:S(2)}) collective-permute-start(s16[160,384]{1,0:T(8,128)(2,1)S(1)} %get-tuple-element.12), channel_id=1, source_target_pairs={{0,4},{4,0},{8,12},{12,8},{1,5},{5,1},{9,13},{13,9},{2,6},{6,2},{1... | collective-permute-start | bytes 368648 | tf_op jit(solution)/shard_map/ppermute | solution.py:233
  4.1 6.6 %collective-permute-start.1 = (s16[160,384]{1,0:T(8,128)(2,1)S(1)}, s16[160,384]{1,0:T(8,128)(2,1)S(1)}, u32[]{:S(2)}, u32[]{:S(2)}) collective-permute-start(s16[160,384]{1,0:T(8,128)(2,1)S(1)} %add.6.own), channel_id=1, source_target_pairs={{0,8},{4,12},{8,0},{12,4},{1,9},{5,13},{9,1},{13,5},{2,10},{6,14},... | collective-permute-start | bytes 368648 | tf_op jit(solution)/shard_map/ppermute | solution.py:233
  7.0 0.7 %copy-start = (s32[4,2]{0,1:T(2,128)S(1)}, s32[4,2]{0,1:T(2,128)}, u32[]{:S(2)}) copy-start(s32[4,2]{0,1:T(2,128)} %param.9) | copy-start | bytes 100
  10.7 1.4 %collective-permute-start.2 = (s16[160,384]{1,0:T(8,128)(2,1)S(1)}, s16[160,384]{1,0:T(8,128)(2,1)S(1)}, u32[]{:S(2)}, u32[]{:S(2)}) collective-permute-start(s16[160,384]{1,0:T(8,128)(2,1)S(1)} %add.7.own), channel_id=1, source_target_pairs={{0,4},{4,0},{8,12},{12,8},{1,5},{5,1},{9,13},{13,9},{2,6},{6,2},{1... | collective-permute-start | bytes 368648 | tf_op jit(solution)/shard_map/ppermute | solution.py:233

commit v4 on v3

--- a/solution.py
+++ b/solution.py
@@ -165,9 +165,11 @@
 
 
 def image_kernel(
-    facet_steps, own, other, left, right, out, row_re, row_im, col_re, col_im, field_re, field_im, total, *, count, group, padded, lanes
+    facet_steps, own, other, left, right, out, row_re, row_im, col_re, col_im, field_re, field_im, stack, total,
+    *, count, step_pairs, padded, lanes
 ):
     me = lax.axis_index("mod")
+    double = 2 * P_SIZE
     odd = lax.rem(me, 2) == 1
     mine = own[...].astype(I32)
     theirs = other[...].astype(I32)
@@ -178,53 +180,89 @@
     radius = along_y * along_y + along_x * along_x
     edge = P_SIZE * 28 // 100
     inside = (radius <= P_SIZE * P_SIZE) & (radius >= edge * edge)
-    field_re[...] = jnp.where(inside, wave_re, 0.0)
-    field_im[...] = jnp.where(inside, wave_im, 0.0)
+    for target, wave in ((field_re, wave_re), (field_im, wave_im)):
+        kept = jnp.where(inside, wave, 0.0)[:, :P_SIZE]
+        target[...] = jnp.concatenate([kept, kept], 1)
     base = P_SIZE // 128 * 128
     tilt_row = mine[HALF - 1 : HALF, base : base + 128]
     steps = (tilt_row - CENTRE) * iota((P_SIZE, 128), 0)
-    cos_rows, sin_rows = cos_sin(centred(steps.astype(F32) * (1.0 / FINE)))
-    for point in range(count):
-        place = P_SIZE - base + point
-        row_re[point] = jnp.broadcast_to(cos_rows[:, place : place + 1], (P_SIZE, 128))
-        row_im[point] = jnp.broadcast_to(sin_rows[:, place : place + 1], (P_SIZE, 128))
-    for point in range(count):
-        tilt_col = mine[point : point + 1, lanes - 1 : lanes]
-        steps = (tilt_col - CENTRE) * iota((8, lanes), 1) + facet_steps[...]
-        turn_re, turn_im = cos_sin(centred(steps.astype(F32) * (1.0 / FINE)))
-        col_re[point] = turn_re
-        col_im[point] = turn_im
+    turned = cos_sin(centred(steps.astype(F32) * (1.0 / FINE)))
+    lane = iota((P_SIZE, 128), 1)
+    for pair in range(count // 2):
+        place = P_SIZE - base + 2 * pair
+        for target, wave in zip((row_re, row_im), turned):
+            one = jnp.broadcast_to(wave[:, place : place + 1], (P_SIZE, 128))
+            two = jnp.broadcast_to(wave[:, place + 1 : place + 2], (P_SIZE, 128))
+            target[pair] = jnp.concatenate([one, jnp.where(lane < P_SIZE - base, one, two), two], 1)
+        parts = []
+        for point in (2 * pair, 2 * pair + 1):
+            tilt_col = mine[point : point + 1, lanes - 1 : lanes]
+            steps = (tilt_col - CENTRE) * iota((8, lanes), 1) + facet_steps[...]
+            parts.append(cos_sin(centred(steps.astype(F32) * (1.0 / FINE))))
+        for target, one, two in zip((col_re, col_im), *parts):
+            target[pair] = jnp.concatenate([one[:, :P_SIZE], two[:, :P_SIZE]], 1)
+    rows = 2 * padded
+    period = total.shape[1] // 128
+    steps = count // (2 * step_pairs)
     total[...] = jnp.zeros_like(total)
 
-    def one_group(index, carry):
-        copies = lanes // 128
-        stacked = []
-        for member in range(group):
-            point = index * group + member
-            turn_re = jnp.concatenate([row_re[point]] * copies, 1)
-            turn_im = jnp.concatenate([row_im[point]] * copies, 1)
-            wide_re, wide_im = field_re[...], field_im[...]
-            moved_re = (wide_re * turn_re - wide_im * turn_im).astype(BF16)
-            moved_im = (wide_re * turn_im + wide_im * turn_re).astype(BF16)
-            half = jnp.dot(left[...], jnp.concatenate([moved_re, moved_im], 1), preferred_element_type=F32)
-            parts_re, parts_im = [], []
+    def row_product(pair):
+        turns = []
+        for source in (row_re, row_im):
+            one, mix, two = (source[pair, :, tile * 128 : tile * 128 + 128] for tile in range(3))
+            turns.append(jnp.concatenate([one] * (base // 128) + [mix] + [two] * (base // 128), 1))
+        turn_re, turn_im = turns
+        wide_re, wide_im = field_re[...], field_im[...]
+        moved_re = (wide_re * turn_re - wide_im * turn_im).astype(BF16)
+        moved_im = (wide_re * turn_im + wide_im * turn_re).astype(BF16)
+        return jnp.dot(left[...], jnp.concatenate([moved_re, moved_im], 1), preferred_element_type=F32)
+
+    def turned_pieces(pair, product, quadrant):
+        turn_re = col_re[pair, quadrant : quadrant + 1, :]
+        turn_im = col_im[pair, quadrant : quadrant + 1, :]
+        piece = product[quadrant * padded : (quadrant + 1) * padded]
+        piece_re, piece_im = piece[:, :double], piece[:, double:]
+        return (
+            (piece_re * turn_re - piece_im * turn_im).astype(BF16),
+            (piece_re * turn_im + piece_im * turn_re).astype(BF16),
+        )
+
+    def keep_rows(place, pieces):
+        for member in range(2):
+            span = slice(member * P_SIZE, (member + 1) * P_SIZE)
+            for part in range(2):
+                start = (2 * place + member) * rows + part * padded
+                stack[start : start + padded, :] = jnp.concatenate([piece[part][:, span] for piece in pieces], 1)
+
+    def image_chunk(start, stop):
+        image = lax.dot_general(right[...], stack[start:stop, :], (((1,), (1,)), ((), ())), preferred_element_type=F32)
+        for tile in range((stop - start) // 128):
+            part = image[:, tile * 128 : tile * 128 + 128]
+            target = (start // 128 + tile) % period * 128
+            total[:, target : target + 128] += part * part
+
+    def one_step(index, carry):
+        chunks = [(start, min(start + 256, 2 * step_pairs * rows)) for start in range(0, 2 * step_pairs * rows, 256)]
+        for place in range(step_pairs):
+            pair = index * step_pairs + place
+            ready = [chunk for chunk in chunks if chunk[1] <= 2 * place * rows]
+            chunks = chunks[len(ready) :]
+            product = row_product(pair)
+            pieces = []
             for quadrant in range(4):
-                piece = half[quadrant * padded : (quadrant + 1) * padded]
-                piece_re, piece_im = piece[:, :lanes], piece[:, lanes:]
-                turn_re = col_re[point, quadrant : quadrant + 1, :]
-                turn_im = col_im[point, quadrant : quadrant + 1, :]
-                parts_re.append((piece_re * turn_re - piece_im * turn_im).astype(BF16)[:, :P_SIZE])
-                parts_im.append((piece_re * turn_im + piece_im * turn_re).astype(BF16)[:, :P_SIZE])
-            stacked += [jnp.concatenate(parts_re, 1), jnp.concatenate(parts_im, 1)]
-        image = lax.dot_general(
-            right[...], jnp.concatenate(stacked, 0), (((1,), (1,)), ((), ())), preferred_element_type=F32
-        )
-        total[...] += image * image
+                if ready:
+                    image_chunk(*ready.pop(0))
+                pieces.append(turned_pieces(pair, product, quadrant))
+            for chunk in ready:
+                image_chunk(*chunk)
+            keep_rows(place, pieces)
+        for chunk in chunks:
+            image_chunk(*chunk)
         return carry
 
-    lax.fori_loop(0, count // group, one_group, 0, unroll=min(count // group, 2))
+    lax.fori_loop(0, steps, one_step, 0)
     folded = total[:, :padded]
-    for block in range(1, 2 * group):
+    for block in range(1, period * 128 // padded):
         folded = folded + total[:, block * padded : (block + 1) * padded]
     out[0] = folded.T[: out.shape[1]] * (4.0 / count)
 
@@ -237,7 +275,7 @@
     peers = lax.axis_size("mod")
     layers, band, width = screens.shape
     count = tilt_steps.shape[0] * peers
-    group = math.gcd(count, 4)
+    step_pairs = math.gcd(count // 2, 4)
     rows = PAD // peers
     padded = round_up(rows, 16)
     lanes = round_up(P_SIZE + count + 1, 128)
@@ -283,18 +321,19 @@
         step *= 2
     other = swapped(own, peers, 1)
     return pl.pallas_call(
-        functools.partial(image_kernel, count=count, group=group, padded=padded, lanes=lanes),
+        functools.partial(image_kernel, count=count, step_pairs=step_pairs, padded=padded, lanes=lanes),
         out_shape=jax.ShapeDtypeStruct((1, rows, PAD), F32),
         in_specs=[vmem, vmem, vmem, vmem, vmem],
         out_specs=vmem,
         scratch_shapes=[
-            pltpu.VMEM((count, P_SIZE, 128), F32),
-            pltpu.VMEM((count, P_SIZE, 128), F32),
-            pltpu.VMEM((count, 8, lanes), F32),
-            pltpu.VMEM((count, 8, lanes), F32),
-            pltpu.VMEM((P_SIZE, lanes), F32),
-            pltpu.VMEM((P_SIZE, lanes), F32),
-            pltpu.VMEM((PAD, 2 * group * padded), F32),
+            pltpu.VMEM((count // 2, P_SIZE, 384), F32),
+            pltpu.VMEM((count // 2, P_SIZE, 384), F32),
+            pltpu.VMEM((count // 2, 8, 2 * P_SIZE), F32),
+            pltpu.VMEM((count // 2, 8, 2 * P_SIZE), F32),
+            pltpu.VMEM((P_SIZE, 2 * P_SIZE), F32),
+            pltpu.VMEM((P_SIZE, 2 * P_SIZE), F32),
+            pltpu.VMEM((4 * step_pairs * padded, 4 * P_SIZE), BF16),
+            pltpu.VMEM((PAD, math.lcm(padded, 128)), F32),
         ],
         compiler_params=params,
         name="detector_rows",

time: 24 us -> 23.2 us (0.967)
  Pallas kernels: 15.5 us -> 14.7 us
    pallas_call x1, Pallas kernels: 11.7 us -> 10.9 us  [shards(): pl.pallas_call(functools.partial(image_kernel, count=count, step_pairs=st...]
where the time goes in v4:
time: 23.2 us; the launch traced here: 23.1 us
  Pallas kernels  14.7 us (63%)
  waiting for transfers between devices  4.07 us (18%)
  starting transfers between devices  3.53 us (15%)
  local copies, waits for them, and re-layouts  0.68 us (3%)
    pallas_call x1, Pallas kernels, shards(): pl.pallas_call(functools.partial(image_kernel, count=count, step_pairs=st...  10.9 us
    ppermute x3, waiting for transfers between devices, swapped(): return lax.ppermute(values, 'mod', [(i, i ^ step) for i in range(peers)])  4.07 us
    ppermute x3, starting transfers between devices, swapped(): return lax.ppermute(values, 'mod', [(i, i ^ step) for i in range(peers)])  3.53 us
    pallas_call x1, Pallas kernels, shards(): pl.pallas_call(functools.partial(phase_kernel, lanes=lanes), out_shape=(p...  2.57 us
    pallas_call x1, Pallas kernels, shards(): pl.pallas_call(functools.partial(table_kernel, rows=rows, padded=padded,...  1.17 us
    unnamed x2, local copies, waits for them, and re-layouts  0.68 us
  transfers between devices with their start and end apart: 3, of which 3 were waited for; matrix products, arithmetic and copies ran while one was open for 0% of the time, Pallas kernels for 5%

profile of v4, /device:TPU:0, one launch (start us, length us, event | category | flops | bytes accessed | tf_op | source)
XLA Modules:
  0.0 23.1 jit_solution(8052436391352037694)
XLA Ops:
  0.0 2.6 %phase_parts.1 = (s16[160,384]{1,0:T(8,128)(2,1)S(1)}, s16[160,384]{1,0:T(8,128)(2,1)S(1)}) custom-call(s32[1,2,4]{2,1,0:T(2,128)} %bitcast.4, s32[1,2,4]{2,1,0:T(2,128)} %bitcast.5, s32[2,2]{1,0:T(2,128)} %tilt_hbm.1, f32[4,128,512]{2,1,0:T(8,128)} %screens_hbm.1), custom_call_target="tpu_custom_call" | custom-call | tf_op jit(solution)/shard_map/phase_parts/pallas_call | solution.py:286
  2.6 0.5 %collective-permute-start = (s16[160,384]{1,0:T(8,128)(2,1)S(1)}, s16[160,384]{1,0:T(8,128)(2,1)S(1)}, u32[]{:S(2)}, u32[]{:S(2)}) collective-permute-start(s16[160,384]{1,0:T(8,128)(2,1)S(1)} %get-tuple-element.12), channel_id=1, source_target_pairs={{0,4},{4,0},{8,12},{12,8},{1,5},{5,1},{9,13},{13,9},{2,6},{6,2},{1... | collective-permute-start | bytes 368648 | tf_op jit(solution)/shard_map/ppermute | solution.py:271
  3.1 1.0 %collective-permute-done = s16[160,384]{1,0:T(8,128)(2,1)S(1)} collective-permute-done((s16[160,384]{1,0:T(8,128)(2,1)S(1)}, s16[160,384]{1,0:T(8,128)(2,1)S(1)}, u32[]{:S(2)}, u32[]{:S(2)}) %collective-permute-start) | collective-permute-done | bytes 122912 | tf_op jit(solution)/shard_map/ppermute | solution.py:271
  4.1 2.9 %collective-permute-start.1 = (s16[160,384]{1,0:T(8,128)(2,1)S(1)}, s16[160,384]{1,0:T(8,128)(2,1)S(1)}, u32[]{:S(2)}, u32[]{:S(2)}) collective-permute-start(s16[160,384]{1,0:T(8,128)(2,1)S(1)} %add.6.own), channel_id=1, source_target_pairs={{0,8},{4,12},{8,0},{12,4},{1,9},{5,13},{9,1},{13,5},{2,10},{6,14},... | collective-permute-start | bytes 368648 | tf_op jit(solution)/shard_map/ppermute | solution.py:271
  7.0 0.0 copy-start
  7.0 0.7 %copy-done = s32[4,2]{0,1:T(2,128)S(1)} copy-done((s32[4,2]{0,1:T(2,128)S(1)}, s32[4,2]{0,1:T(2,128)}, u32[]{:S(2)}) %copy-start) | copy-done | bytes 56
  7.7 1.2 %half_band_tables.1 = (bf16[640,320]{1,0:T(8,128)(2,1)S(1)}, bf16[640,1280]{1,0:T(8,128)(2,1)S(1)}, s32[8,384]{1,0:T(8,128)S(1)}, s16[160,384]{1,0:T(8,128)(2,1)S(1)}) custom-call(s32[2,4]{1,0:T(2,128)S(1)} %bitcast.3, s16[160,384]{1,0:T(8,128)(2,1)S(1)} %add.6.own), custom_call_target="tpu_custom_call" | custom-call | flops 5000000000 | bytes 20000000 | tf_op jit(solution)/shard_map/half_band_tables/pallas_call | solution.py:303
  8.9 1.8 %collective-permute-done.1 = s16[160,384]{1,0:T(8,128)(2,1)S(1)} collective-permute-done((s16[160,384]{1,0:T(8,128)(2,1)S(1)}, s16[160,384]{1,0:T(8,128)(2,1)S(1)}, u32[]{:S(2)}, u32[]{:S(2)}) %collective-permute-start.1) | collective-permute-done | bytes 122912 | tf_op jit(solution)/shard_map/ppermute | solution.py:271
  10.7 0.1 collective-permute-start.2
  10.8 1.3 %collective-permute-done.2.other = s16[160,384]{1,0:T(8,128)(2,1)S(1)} collective-permute-done((s16[160,384]{1,0:T(8,128)(2,1)S(1)}, s16[160,384]{1,0:T(8,128)(2,1)S(1)}, u32[]{:S(2)}, u32[]{:S(2)}) %collective-permute-start.2) | collective-permute-done | bytes 122912 | tf_op jit(solution)/shard_map/ppermute | solution.py:271
  12.1 10.9 %detector_rows.1 = f32[1,160,640]{2,1,0:T(8,128)} custom-call(s32[8,384]{1,0:T(8,128)S(1)} %get-tuple-element.13.facet_steps, s16[160,384]{1,0:T(8,128)(2,1)S(1)} %add.7.own, s16[160,384]{1,0:T(8,128)(2,1)S(1)} %collective-permute-done.2.other, bf16[640,320]{1,0:T(8,128)(2,1)S(1)} %get-tuple-element.15.left, bf16[640,1280]{1,0:T(8,128)(2,1)S(1)} %get-tuple-element.16.right), custom_call_target="tpu_custom_call" | custom-call | tf_op jit(solution)/shard_map/detector_rows/pallas_call | solution.py:323
  (2 shorter events, 0.1 us)
Async XLA Ops:
  2.6 1.5 %collective-permute-start = (s16[160,384]{1,0:T(8,128)(2,1)S(1)}, s16[160,384]{1,0:T(8,128)(2,1)S(1)}, u32[]{:S(2)}, u32[]{:S(2)}) collective-permute-start(s16[160,384]{1,0:T(8,128)(2,1)S(1)} %get-tuple-element.12), channel_id=1, source_target_pairs={{0,4},{4,0},{8,12},{12,8},{1,5},{5,1},{9,13},{13,9},{2,6},{6,2},{1... | collective-permute-start | bytes 368648 | tf_op jit(solution)/shard_map/ppermute | solution.py:271
  4.1 6.6 %collective-permute-start.1 = (s16[160,384]{1,0:T(8,128)(2,1)S(1)}, s16[160,384]{1,0:T(8,128)(2,1)S(1)}, u32[]{:S(2)}, u32[]{:S(2)}) collective-permute-start(s16[160,384]{1,0:T(8,128)(2,1)S(1)} %add.6.own), channel_id=1, source_target_pairs={{0,8},{4,12},{8,0},{12,4},{1,9},{5,13},{9,1},{13,5},{2,10},{6,14},... | collective-permute-start | bytes 368648 | tf_op jit(solution)/shard_map/ppermute | solution.py:271
  7.0 0.7 %copy-start = (s32[4,2]{0,1:T(2,128)S(1)}, s32[4,2]{0,1:T(2,128)}, u32[]{:S(2)}) copy-start(s32[4,2]{0,1:T(2,128)} %param.9) | copy-start | bytes 100
  10.7 1.4 %collective-permute-start.2 = (s16[160,384]{1,0:T(8,128)(2,1)S(1)}, s16[160,384]{1,0:T(8,128)(2,1)S(1)}, u32[]{:S(2)}, u32[]{:S(2)}) collective-permute-start(s16[160,384]{1,0:T(8,128)(2,1)S(1)} %add.7.own), channel_id=1, source_target_pairs={{0,4},{4,0},{8,12},{12,8},{1,5},{5,1},{9,13},{13,9},{2,6},{6,2},{1... | collective-permute-start | bytes 368648 | tf_op jit(solution)/shard_map/ppermute | solution.py:271

commit v5 on v4

--- a/solution.py
+++ b/solution.py
@@ -83,14 +83,14 @@
         part = frac[0, 1, layer].astype(F32) * (1.0 / 16.0)
         large[layer].wait()
         rows = screens[layer]
-        here = pltpu.roll(rows, lax.rem(width - start, width), 1)[:, :lanes]
-        after = pltpu.roll(rows, width - 1 - start, 1)[:, :lanes]
-        mixed = here * (1.0 - part) + after * part
+        mixed = rows * (1.0 - part) + pltpu.roll(rows, width - 1, 1) * part
+        mixed = pltpu.roll(mixed, lax.rem(width - start, width), 1)[:, :lanes]
         top = mixed.astype(BF16)
         high.append(top)
         low.append((mixed - top.astype(F32)).astype(BF16))
-    total = jnp.dot(pick, jnp.concatenate(high, 0), preferred_element_type=F32)
-    total = total + jnp.dot(pick, jnp.concatenate(low, 0), preferred_element_type=F32)
+    both = jnp.concatenate([jnp.concatenate(high, 0), jnp.concatenate(low, 0)], 1)
+    both = jnp.dot(pick, both, preferred_element_type=F32)
+    total = both[:, :lanes] + both[:, lanes:]
     coded = jnp.floor(total * (65536.0 / 6.283185307179586) + 0.5).astype(I32)
     coded = lax.shift_right_arithmetic(lax.shift_left(coded, 16), 16)
     row = iota((HALF, lanes), 0)
@@ -188,7 +188,8 @@
     steps = (tilt_row - CENTRE) * iota((P_SIZE, 128), 0)
     turned = cos_sin(centred(steps.astype(F32) * (1.0 / FINE)))
     lane = iota((P_SIZE, 128), 1)
-    for pair in range(count // 2):
+
+    def prepare(pair):
         place = P_SIZE - base + 2 * pair
         for target, wave in zip((row_re, row_im), turned):
             one = jnp.broadcast_to(wave[:, place : place + 1], (P_SIZE, 128))
@@ -201,10 +202,13 @@
             parts.append(cos_sin(centred(steps.astype(F32) * (1.0 / FINE))))
         for target, one, two in zip((col_re, col_im), *parts):
             target[pair] = jnp.concatenate([one[:, :P_SIZE], two[:, :P_SIZE]], 1)
+
     rows = 2 * padded
     period = total.shape[1] // 128
     steps = count // (2 * step_pairs)
     total[...] = jnp.zeros_like(total)
+    for pair in range(1 if steps == 1 else count // 2):
+        prepare(pair)
 
     def row_product(pair):
         turns = []
@@ -255,12 +259,17 @@
                 pieces.append(turned_pieces(pair, product, quadrant))
             for chunk in ready:
                 image_chunk(*chunk)
+            if steps == 1 and place + 1 < step_pairs:
+                prepare(place + 1)
             keep_rows(place, pieces)
         for chunk in chunks:
             image_chunk(*chunk)
         return carry
 
-    lax.fori_loop(0, steps, one_step, 0)
+    if steps == 1:
+        one_step(0, 0)
+    else:
+        lax.fori_loop(0, steps, one_step, 0)
     folded = total[:, :padded]
     for block in range(1, period * 128 // padded):
         folded = folded + total[:, block * padded : (block + 1) * padded]

time: 23.2 us -> 23.1 us (level)
  no operation moved by 1% of the time
where the time goes in v5:
time: 23.1 us; the launch traced here: 23 us
  Pallas kernels  14.6 us (63%)
  waiting for transfers between devices  4.07 us (18%)
  starting transfers between devices  3.53 us (15%)
  local copies, waits for them, and re-layouts  0.68 us (3%)
    pallas_call x1, Pallas kernels, shards(): pl.pallas_call(functools.partial(image_kernel, count=count, step_pairs=st...  10.9 us
    ppermute x3, waiting for transfers between devices, swapped(): return lax.ppermute(values, 'mod', [(i, i ^ step) for i in range(peers)])  4.07 us
    ppermute x3, starting transfers between devices, swapped(): return lax.ppermute(values, 'mod', [(i, i ^ step) for i in range(peers)])  3.53 us
    pallas_call x1, Pallas kernels, shards(): pl.pallas_call(functools.partial(phase_kernel, lanes=lanes), out_shape=(p...  2.5 us
    pallas_call x1, Pallas kernels, shards(): pl.pallas_call(functools.partial(table_kernel, rows=rows, padded=padded,...  1.17 us
    unnamed x2, local copies, waits for them, and re-layouts  0.68 us
  transfers between devices with their start and end apart: 3, of which 3 were waited for; matrix products, arithmetic and copies ran while one was open for 0% of the time, Pallas kernels for 5%

profile of v5, /device:TPU:0, one launch (start us, length us, event | category | flops | bytes accessed | tf_op | source)
XLA Modules:
  0.0 23.0 jit_solution(571327013064142224)
XLA Ops:
  0.0 2.5 %phase_parts.1 = (s16[160,384]{1,0:T(8,128)(2,1)S(1)}, s16[160,384]{1,0:T(8,128)(2,1)S(1)}) custom-call(s32[1,2,4]{2,1,0:T(2,128)} %bitcast.4, s32[1,2,4]{2,1,0:T(2,128)} %bitcast.5, s32[2,2]{1,0:T(2,128)} %tilt_hbm.1, f32[4,128,512]{2,1,0:T(8,128)} %screens_hbm.1), custom_call_target="tpu_custom_call" | custom-call | tf_op jit(solution)/shard_map/phase_parts/pallas_call | solution.py:295
  2.5 0.5 %collective-permute-start = (s16[160,384]{1,0:T(8,128)(2,1)S(1)}, s16[160,384]{1,0:T(8,128)(2,1)S(1)}, u32[]{:S(2)}, u32[]{:S(2)}) collective-permute-start(s16[160,384]{1,0:T(8,128)(2,1)S(1)} %get-tuple-element.12), channel_id=1, source_target_pairs={{0,4},{4,0},{8,12},{12,8},{1,5},{5,1},{9,13},{13,9},{2,6},{6,2},{1... | collective-permute-start | bytes 368648 | tf_op jit(solution)/shard_map/ppermute | solution.py:280
  3.0 1.0 %collective-permute-done = s16[160,384]{1,0:T(8,128)(2,1)S(1)} collective-permute-done((s16[160,384]{1,0:T(8,128)(2,1)S(1)}, s16[160,384]{1,0:T(8,128)(2,1)S(1)}, u32[]{:S(2)}, u32[]{:S(2)}) %collective-permute-start) | collective-permute-done | bytes 122912 | tf_op jit(solution)/shard_map/ppermute | solution.py:280
  4.0 2.9 %collective-permute-start.1 = (s16[160,384]{1,0:T(8,128)(2,1)S(1)}, s16[160,384]{1,0:T(8,128)(2,1)S(1)}, u32[]{:S(2)}, u32[]{:S(2)}) collective-permute-start(s16[160,384]{1,0:T(8,128)(2,1)S(1)} %add.6.own), channel_id=1, source_target_pairs={{0,8},{4,12},{8,0},{12,4},{1,9},{5,13},{9,1},{13,5},{2,10},{6,14},... | collective-permute-start | bytes 368648 | tf_op jit(solution)/shard_map/ppermute | solution.py:280
  7.0 0.0 copy-start
  7.0 0.7 %copy-done = s32[4,2]{0,1:T(2,128)S(1)} copy-done((s32[4,2]{0,1:T(2,128)S(1)}, s32[4,2]{0,1:T(2,128)}, u32[]{:S(2)}) %copy-start) | copy-done | bytes 56
  7.7 1.2 %half_band_tables.1 = (bf16[640,320]{1,0:T(8,128)(2,1)S(1)}, bf16[640,1280]{1,0:T(8,128)(2,1)S(1)}, s32[8,384]{1,0:T(8,128)S(1)}, s16[160,384]{1,0:T(8,128)(2,1)S(1)}) custom-call(s32[2,4]{1,0:T(2,128)S(1)} %bitcast.3, s16[160,384]{1,0:T(8,128)(2,1)S(1)} %add.6.own), custom_call_target="tpu_custom_call" | custom-call | flops 5000000000 | bytes 20000000 | tf_op jit(solution)/shard_map/half_band_tables/pallas_call | solution.py:312
  8.8 1.8 %collective-permute-done.1 = s16[160,384]{1,0:T(8,128)(2,1)S(1)} collective-permute-done((s16[160,384]{1,0:T(8,128)(2,1)S(1)}, s16[160,384]{1,0:T(8,128)(2,1)S(1)}, u32[]{:S(2)}, u32[]{:S(2)}) %collective-permute-start.1) | collective-permute-done | bytes 122912 | tf_op jit(solution)/shard_map/ppermute | solution.py:280
  10.7 0.1 collective-permute-start.2
  10.7 1.3 %collective-permute-done.2.other = s16[160,384]{1,0:T(8,128)(2,1)S(1)} collective-permute-done((s16[160,384]{1,0:T(8,128)(2,1)S(1)}, s16[160,384]{1,0:T(8,128)(2,1)S(1)}, u32[]{:S(2)}, u32[]{:S(2)}) %collective-permute-start.2) | collective-permute-done | bytes 122912 | tf_op jit(solution)/shard_map/ppermute | solution.py:280
  12.1 10.9 %detector_rows.1 = f32[1,160,640]{2,1,0:T(8,128)} custom-call(s32[8,384]{1,0:T(8,128)S(1)} %get-tuple-element.13.facet_steps, s16[160,384]{1,0:T(8,128)(2,1)S(1)} %add.7.own, s16[160,384]{1,0:T(8,128)(2,1)S(1)} %collective-permute-done.2.other, bf16[640,320]{1,0:T(8,128)(2,1)S(1)} %get-tuple-element.15.left, bf16[640,1280]{1,0:T(8,128)(2,1)S(1)} %get-tuple-element.16.right), custom_call_target="tpu_custom_call" | custom-call | tf_op jit(solution)/shard_map/detector_rows/pallas_call | solution.py:332
  (2 shorter events, 0.1 us)
Async XLA Ops:
  2.5 1.5 %collective-permute-start = (s16[160,384]{1,0:T(8,128)(2,1)S(1)}, s16[160,384]{1,0:T(8,128)(2,1)S(1)}, u32[]{:S(2)}, u32[]{:S(2)}) collective-permute-start(s16[160,384]{1,0:T(8,128)(2,1)S(1)} %get-tuple-element.12), channel_id=1, source_target_pairs={{0,4},{4,0},{8,12},{12,8},{1,5},{5,1},{9,13},{13,9},{2,6},{6,2},{1... | collective-permute-start | bytes 368648 | tf_op jit(solution)/shard_map/ppermute | solution.py:280
  4.0 6.6 %collective-permute-start.1 = (s16[160,384]{1,0:T(8,128)(2,1)S(1)}, s16[160,384]{1,0:T(8,128)(2,1)S(1)}, u32[]{:S(2)}, u32[]{:S(2)}) collective-permute-start(s16[160,384]{1,0:T(8,128)(2,1)S(1)} %add.6.own), channel_id=1, source_target_pairs={{0,8},{4,12},{8,0},{12,4},{1,9},{5,13},{9,1},{13,5},{2,10},{6,14},... | collective-permute-start | bytes 368648 | tf_op jit(solution)/shard_map/ppermute | solution.py:280
  7.0 0.7 %copy-start = (s32[4,2]{0,1:T(2,128)S(1)}, s32[4,2]{0,1:T(2,128)}, u32[]{:S(2)}) copy-start(s32[4,2]{0,1:T(2,128)} %param.9) | copy-start | bytes 100
  10.7 1.4 %collective-permute-start.2 = (s16[160,384]{1,0:T(8,128)(2,1)S(1)}, s16[160,384]{1,0:T(8,128)(2,1)S(1)}, u32[]{:S(2)}, u32[]{:S(2)}) collective-permute-start(s16[160,384]{1,0:T(8,128)(2,1)S(1)} %add.7.own), channel_id=1, source_target_pairs={{0,4},{4,0},{8,12},{12,8},{1,5},{5,1},{9,13},{13,9},{2,6},{6,2},{1... | collective-permute-start | bytes 368648 | tf_op jit(solution)/shard_map/ppermute | solution.py:280

commit v6 on v5

--- a/solution.py
+++ b/solution.py
@@ -175,8 +175,8 @@
     theirs = other[...].astype(I32)
     coded = jnp.concatenate([jnp.where(odd, theirs, mine), jnp.where(odd, mine, theirs)], 0)
     wave_re, wave_im = cos_sin(coded.astype(F32) * (1.0 / 65536.0))
-    along_y = 2 * iota((P_SIZE, lanes), 0) - (P_SIZE - 1)
-    along_x = 2 * iota((P_SIZE, lanes), 1) - (P_SIZE - 1)
+    along_y = 2 * iota((P_SIZE, 1), 0) - (P_SIZE - 1)
+    along_x = 2 * iota((1, lanes), 1) - (P_SIZE - 1)
     radius = along_y * along_y + along_x * along_x
     edge = P_SIZE * 28 // 100
     inside = (radius <= P_SIZE * P_SIZE) & (radius >= edge * edge)
@@ -257,11 +257,11 @@
                 if ready:
                     image_chunk(*ready.pop(0))
                 pieces.append(turned_pieces(pair, product, quadrant))
-            for chunk in ready:
-                image_chunk(*chunk)
             if steps == 1 and place + 1 < step_pairs:
                 prepare(place + 1)
             keep_rows(place, pieces)
+            for chunk in ready:
+                image_chunk(*chunk)
         for chunk in chunks:
             image_chunk(*chunk)
         return carry

time: 23.1 us -> 23.1 us (level)
  no operation moved by 1% of the time
where the time goes in v6:
time: 23.1 us; the launch traced here: 23 us
  Pallas kernels  14.6 us (63%)
  waiting for transfers between devices  4.07 us (18%)
  starting transfers between devices  3.53 us (15%)
  local copies, waits for them, and re-layouts  0.68 us (3%)
    pallas_call x1, Pallas kernels, shards(): pl.pallas_call(functools.partial(image_kernel, count=count, step_pairs=st...  10.9 us
    ppermute x3, waiting for transfers between devices, swapped(): return lax.ppermute(values, 'mod', [(i, i ^ step) for i in range(peers)])  4.07 us
    ppermute x3, starting transfers between devices, swapped(): return lax.ppermute(values, 'mod', [(i, i ^ step) for i in range(peers)])  3.53 us
    pallas_call x1, Pallas kernels, shards(): pl.pallas_call(functools.partial(phase_kernel, lanes=lanes), out_shape=(p...  2.5 us
    pallas_call x1, Pallas kernels, shards(): pl.pallas_call(functools.partial(table_kernel, rows=rows, padded=padded,...  1.17 us
    unnamed x2, local copies, waits for them, and re-layouts  0.68 us
  transfers between devices with their start and end apart: 3, of which 3 were waited for; matrix products, arithmetic and copies ran while one was open for 0% of the time, Pallas kernels for 5%

profile of v6, /device:TPU:0, one launch (start us, length us, event | category | flops | bytes accessed | tf_op | source)
XLA Modules:
  0.0 23.0 jit_solution(571327013064142224)
XLA Ops:
  0.0 2.5 %phase_parts.1 = (s16[160,384]{1,0:T(8,128)(2,1)S(1)}, s16[160,384]{1,0:T(8,128)(2,1)S(1)}) custom-call(s32[1,2,4]{2,1,0:T(2,128)} %bitcast.4, s32[1,2,4]{2,1,0:T(2,128)} %bitcast.5, s32[2,2]{1,0:T(2,128)} %tilt_hbm.1, f32[4,128,512]{2,1,0:T(8,128)} %screens_hbm.1), custom_call_target="tpu_custom_call" | custom-call | tf_op jit(solution)/shard_map/phase_parts/pallas_call | solution.py:295
  2.5 0.5 %collective-permute-start = (s16[160,384]{1,0:T(8,128)(2,1)S(1)}, s16[160,384]{1,0:T(8,128)(2,1)S(1)}, u32[]{:S(2)}, u32[]{:S(2)}) collective-permute-start(s16[160,384]{1,0:T(8,128)(2,1)S(1)} %get-tuple-element.12), channel_id=1, source_target_pairs={{0,4},{4,0},{8,12},{12,8},{1,5},{5,1},{9,13},{13,9},{2,6},{6,2},{1... | collective-permute-start | bytes 368648 | tf_op jit(solution)/shard_map/ppermute | solution.py:280
  3.0 1.0 %collective-permute-done = s16[160,384]{1,0:T(8,128)(2,1)S(1)} collective-permute-done((s16[160,384]{1,0:T(8,128)(2,1)S(1)}, s16[160,384]{1,0:T(8,128)(2,1)S(1)}, u32[]{:S(2)}, u32[]{:S(2)}) %collective-permute-start) | collective-permute-done | bytes 122912 | tf_op jit(solution)/shard_map/ppermute | solution.py:280
  4.0 2.9 %collective-permute-start.1 = (s16[160,384]{1,0:T(8,128)(2,1)S(1)}, s16[160,384]{1,0:T(8,128)(2,1)S(1)}, u32[]{:S(2)}, u32[]{:S(2)}) collective-permute-start(s16[160,384]{1,0:T(8,128)(2,1)S(1)} %add.6.own), channel_id=1, source_target_pairs={{0,8},{4,12},{8,0},{12,4},{1,9},{5,13},{9,1},{13,5},{2,10},{6,14},... | collective-permute-start | bytes 368648 | tf_op jit(solution)/shard_map/ppermute | solution.py:280
  7.0 0.0 copy-start
  7.0 0.7 %copy-done = s32[4,2]{0,1:T(2,128)S(1)} copy-done((s32[4,2]{0,1:T(2,128)S(1)}, s32[4,2]{0,1:T(2,128)}, u32[]{:S(2)}) %copy-start) | copy-done | bytes 56
  7.7 1.2 %half_band_tables.1 = (bf16[640,320]{1,0:T(8,128)(2,1)S(1)}, bf16[640,1280]{1,0:T(8,128)(2,1)S(1)}, s32[8,384]{1,0:T(8,128)S(1)}, s16[160,384]{1,0:T(8,128)(2,1)S(1)}) custom-call(s32[2,4]{1,0:T(2,128)S(1)} %bitcast.3, s16[160,384]{1,0:T(8,128)(2,1)S(1)} %add.6.own), custom_call_target="tpu_custom_call" | custom-call | flops 5000000000 | bytes 20000000 | tf_op jit(solution)/shard_map/half_band_tables/pallas_call | solution.py:312
  8.8 1.8 %collective-permute-done.1 = s16[160,384]{1,0:T(8,128)(2,1)S(1)} collective-permute-done((s16[160,384]{1,0:T(8,128)(2,1)S(1)}, s16[160,384]{1,0:T(8,128)(2,1)S(1)}, u32[]{:S(2)}, u32[]{:S(2)}) %collective-permute-start.1) | collective-permute-done | bytes 122912 | tf_op jit(solution)/shard_map/ppermute | solution.py:280
  10.7 0.1 collective-permute-start.2
  10.7 1.3 %collective-permute-done.2.other = s16[160,384]{1,0:T(8,128)(2,1)S(1)} collective-permute-done((s16[160,384]{1,0:T(8,128)(2,1)S(1)}, s16[160,384]{1,0:T(8,128)(2,1)S(1)}, u32[]{:S(2)}, u32[]{:S(2)}) %collective-permute-start.2) | collective-permute-done | bytes 122912 | tf_op jit(solution)/shard_map/ppermute | solution.py:280
  12.1 10.9 %detector_rows.1 = f32[1,160,640]{2,1,0:T(8,128)} custom-call(s32[8,384]{1,0:T(8,128)S(1)} %get-tuple-element.13.facet_steps, s16[160,384]{1,0:T(8,128)(2,1)S(1)} %add.7.own, s16[160,384]{1,0:T(8,128)(2,1)S(1)} %collective-permute-done.2.other, bf16[640,320]{1,0:T(8,128)(2,1)S(1)} %get-tuple-element.15.left, bf16[640,1280]{1,0:T(8,128)(2,1)S(1)} %get-tuple-element.16.right), custom_call_target="tpu_custom_call" | custom-call | tf_op jit(solution)/shard_map/detector_rows/pallas_call | solution.py:332
  (2 shorter events, 0.1 us)
Async XLA Ops:
  2.5 1.5 %collective-permute-start = (s16[160,384]{1,0:T(8,128)(2,1)S(1)}, s16[160,384]{1,0:T(8,128)(2,1)S(1)}, u32[]{:S(2)}, u32[]{:S(2)}) collective-permute-start(s16[160,384]{1,0:T(8,128)(2,1)S(1)} %get-tuple-element.12), channel_id=1, source_target_pairs={{0,4},{4,0},{8,12},{12,8},{1,5},{5,1},{9,13},{13,9},{2,6},{6,2},{1... | collective-permute-start | bytes 368648 | tf_op jit(solution)/shard_map/ppermute | solution.py:280
  4.0 6.6 %collective-permute-start.1 = (s16[160,384]{1,0:T(8,128)(2,1)S(1)}, s16[160,384]{1,0:T(8,128)(2,1)S(1)}, u32[]{:S(2)}, u32[]{:S(2)}) collective-permute-start(s16[160,384]{1,0:T(8,128)(2,1)S(1)} %add.6.own), channel_id=1, source_target_pairs={{0,8},{4,12},{8,0},{12,4},{1,9},{5,13},{9,1},{13,5},{2,10},{6,14},... | collective-permute-start | bytes 368648 | tf_op jit(solution)/shard_map/ppermute | solution.py:280
  7.0 0.7 %copy-start = (s32[4,2]{0,1:T(2,128)S(1)}, s32[4,2]{0,1:T(2,128)}, u32[]{:S(2)}) copy-start(s32[4,2]{0,1:T(2,128)} %param.9) | copy-start | bytes 100
  10.7 1.4 %collective-permute-start.2 = (s16[160,384]{1,0:T(8,128)(2,1)S(1)}, s16[160,384]{1,0:T(8,128)(2,1)S(1)}, u32[]{:S(2)}, u32[]{:S(2)}) collective-permute-start(s16[160,384]{1,0:T(8,128)(2,1)S(1)} %add.7.own), channel_id=1, source_target_pairs={{0,4},{4,0},{8,12},{12,8},{1,5},{5,1},{9,13},{13,9},{2,6},{6,2},{1... | collective-permute-start | bytes 368648 | tf_op jit(solution)/shard_map/ppermute | solution.py:280

commit v7 on v5

--- a/solution.py
+++ b/solution.py
@@ -246,7 +246,7 @@
             total[:, target : target + 128] += part * part
 
     def one_step(index, carry):
-        chunks = [(start, min(start + 256, 2 * step_pairs * rows)) for start in range(0, 2 * step_pairs * rows, 256)]
+        chunks = [(start, min(start + 512, 2 * step_pairs * rows)) for start in range(0, 2 * step_pairs * rows, 512)]
         for place in range(step_pairs):
             pair = index * step_pairs + place
             ready = [chunk for chunk in chunks if chunk[1] <= 2 * place * rows]

time: 23.1 us -> 23.1 us (level)
  no operation moved by 1% of the time
where the time goes in v7:
time: 23.1 us; the launch traced here: 23 us
  Pallas kernels  14.6 us (63%)
  waiting for transfers between devices  4.07 us (18%)
  starting transfers between devices  3.53 us (15%)
  local copies, waits for them, and re-layouts  0.68 us (3%)
    pallas_call x1, Pallas kernels, shards(): pl.pallas_call(functools.partial(image_kernel, count=count, step_pairs=st...  10.9 us
    ppermute x3, waiting for transfers between devices, swapped(): return lax.ppermute(values, 'mod', [(i, i ^ step) for i in range(peers)])  4.07 us
    ppermute x3, starting transfers between devices, swapped(): return lax.ppermute(values, 'mod', [(i, i ^ step) for i in range(peers)])  3.53 us
    pallas_call x1, Pallas kernels, shards(): pl.pallas_call(functools.partial(phase_kernel, lanes=lanes), out_shape=(p...  2.5 us
    pallas_call x1, Pallas kernels, shards(): pl.pallas_call(functools.partial(table_kernel, rows=rows, padded=padded,...  1.17 us
    unnamed x2, local copies, waits for them, and re-layouts  0.68 us
  transfers between devices with their start and end apart: 3, of which 3 were waited for; matrix products, arithmetic and copies ran while one was open for 0% of the time, Pallas kernels for 5%

profile of v7, /device:TPU:0, one launch (start us, length us, event | category | flops | bytes accessed | tf_op | source)
XLA Modules:
  0.0 23.0 jit_solution(17093216816211211795)
XLA Ops:
  0.0 2.5 %phase_parts.1 = (s16[160,384]{1,0:T(8,128)(2,1)S(1)}, s16[160,384]{1,0:T(8,128)(2,1)S(1)}) custom-call(s32[1,2,4]{2,1,0:T(2,128)} %bitcast.4, s32[1,2,4]{2,1,0:T(2,128)} %bitcast.5, s32[2,2]{1,0:T(2,128)} %tilt_hbm.1, f32[4,128,512]{2,1,0:T(8,128)} %screens_hbm.1), custom_call_target="tpu_custom_call" | custom-call | tf_op jit(solution)/shard_map/phase_parts/pallas_call | solution.py:295
  2.5 0.5 %collective-permute-start = (s16[160,384]{1,0:T(8,128)(2,1)S(1)}, s16[160,384]{1,0:T(8,128)(2,1)S(1)}, u32[]{:S(2)}, u32[]{:S(2)}) collective-permute-start(s16[160,384]{1,0:T(8,128)(2,1)S(1)} %get-tuple-element.12), channel_id=1, source_target_pairs={{0,4},{4,0},{8,12},{12,8},{1,5},{5,1},{9,13},{13,9},{2,6},{6,2},{1... | collective-permute-start | bytes 368648 | tf_op jit(solution)/shard_map/ppermute | solution.py:280
  3.0 1.0 %collective-permute-done = s16[160,384]{1,0:T(8,128)(2,1)S(1)} collective-permute-done((s16[160,384]{1,0:T(8,128)(2,1)S(1)}, s16[160,384]{1,0:T(8,128)(2,1)S(1)}, u32[]{:S(2)}, u32[]{:S(2)}) %collective-permute-start) | collective-permute-done | bytes 122912 | tf_op jit(solution)/shard_map/ppermute | solution.py:280
  4.0 2.9 %collective-permute-start.1 = (s16[160,384]{1,0:T(8,128)(2,1)S(1)}, s16[160,384]{1,0:T(8,128)(2,1)S(1)}, u32[]{:S(2)}, u32[]{:S(2)}) collective-permute-start(s16[160,384]{1,0:T(8,128)(2,1)S(1)} %add.6.own), channel_id=1, source_target_pairs={{0,8},{4,12},{8,0},{12,4},{1,9},{5,13},{9,1},{13,5},{2,10},{6,14},... | collective-permute-start | bytes 368648 | tf_op jit(solution)/shard_map/ppermute | solution.py:280
  7.0 0.0 copy-start
  7.0 0.7 %copy-done = s32[4,2]{0,1:T(2,128)S(1)} copy-done((s32[4,2]{0,1:T(2,128)S(1)}, s32[4,2]{0,1:T(2,128)}, u32[]{:S(2)}) %copy-start) | copy-done | bytes 56
  7.7 1.2 %half_band_tables.1 = (bf16[640,320]{1,0:T(8,128)(2,1)S(1)}, bf16[640,1280]{1,0:T(8,128)(2,1)S(1)}, s32[8,384]{1,0:T(8,128)S(1)}, s16[160,384]{1,0:T(8,128)(2,1)S(1)}) custom-call(s32[2,4]{1,0:T(2,128)S(1)} %bitcast.3, s16[160,384]{1,0:T(8,128)(2,1)S(1)} %add.6.own), custom_call_target="tpu_custom_call" | custom-call | flops 5000000000 | bytes 20000000 | tf_op jit(solution)/shard_map/half_band_tables/pallas_call | solution.py:312
  8.8 1.8 %collective-permute-done.1 = s16[160,384]{1,0:T(8,128)(2,1)S(1)} collective-permute-done((s16[160,384]{1,0:T(8,128)(2,1)S(1)}, s16[160,384]{1,0:T(8,128)(2,1)S(1)}, u32[]{:S(2)}, u32[]{:S(2)}) %collective-permute-start.1) | collective-permute-done | bytes 122912 | tf_op jit(solution)/shard_map/ppermute | solution.py:280
  10.7 0.1 collective-permute-start.2
  10.7 1.3 %collective-permute-done.2.other = s16[160,384]{1,0:T(8,128)(2,1)S(1)} collective-permute-done((s16[160,384]{1,0:T(8,128)(2,1)S(1)}, s16[160,384]{1,0:T(8,128)(2,1)S(1)}, u32[]{:S(2)}, u32[]{:S(2)}) %collective-permute-start.2) | collective-permute-done | bytes 122912 | tf_op jit(solution)/shard_map/ppermute | solution.py:280
  12.1 10.9 %detector_rows.1 = f32[1,160,640]{2,1,0:T(8,128)} custom-call(s32[8,384]{1,0:T(8,128)S(1)} %get-tuple-element.13.facet_steps, s16[160,384]{1,0:T(8,128)(2,1)S(1)} %add.7.own, s16[160,384]{1,0:T(8,128)(2,1)S(1)} %collective-permute-done.2.other, bf16[640,320]{1,0:T(8,128)(2,1)S(1)} %get-tuple-element.15.left, bf16[640,1280]{1,0:T(8,128)(2,1)S(1)} %get-tuple-element.16.right), custom_call_target="tpu_custom_call" | custom-call | tf_op jit(solution)/shard_map/detector_rows/pallas_call | solution.py:332
  (2 shorter events, 0.1 us)
Async XLA Ops:
  2.5 1.5 %collective-permute-start = (s16[160,384]{1,0:T(8,128)(2,1)S(1)}, s16[160,384]{1,0:T(8,128)(2,1)S(1)}, u32[]{:S(2)}, u32[]{:S(2)}) collective-permute-start(s16[160,384]{1,0:T(8,128)(2,1)S(1)} %get-tuple-element.12), channel_id=1, source_target_pairs={{0,4},{4,0},{8,12},{12,8},{1,5},{5,1},{9,13},{13,9},{2,6},{6,2},{1... | collective-permute-start | bytes 368648 | tf_op jit(solution)/shard_map/ppermute | solution.py:280
  4.0 6.6 %collective-permute-start.1 = (s16[160,384]{1,0:T(8,128)(2,1)S(1)}, s16[160,384]{1,0:T(8,128)(2,1)S(1)}, u32[]{:S(2)}, u32[]{:S(2)}) collective-permute-start(s16[160,384]{1,0:T(8,128)(2,1)S(1)} %add.6.own), channel_id=1, source_target_pairs={{0,8},{4,12},{8,0},{12,4},{1,9},{5,13},{9,1},{13,5},{2,10},{6,14},... | collective-permute-start | bytes 368648 | tf_op jit(solution)/shard_map/ppermute | solution.py:280
  7.0 0.7 %copy-start = (s32[4,2]{0,1:T(2,128)S(1)}, s32[4,2]{0,1:T(2,128)}, u32[]{:S(2)}) copy-start(s32[4,2]{0,1:T(2,128)} %param.9) | copy-start | bytes 100
  10.7 1.4 %collective-permute-start.2 = (s16[160,384]{1,0:T(8,128)(2,1)S(1)}, s16[160,384]{1,0:T(8,128)(2,1)S(1)}, u32[]{:S(2)}, u32[]{:S(2)}) collective-permute-start(s16[160,384]{1,0:T(8,128)(2,1)S(1)} %add.7.own), channel_id=1, source_target_pairs={{0,4},{4,0},{8,12},{12,8},{1,5},{5,1},{9,13},{13,9},{2,6},{6,2},{1... | collective-permute-start | bytes 368648 | tf_op jit(solution)/shard_map/ppermute | solution.py:280
